TPU v7x, 32 devices: a whole 2x2x4 slice. The times are simulated.
32 devices in a mesh: seq: 4 (over y, x), dp: 8 (over z, core).
Axes of the slice: x: 2, y: 2, z: 4, core: 2. Of those that a mesh axis runs over, the one named last changes fastest.
Arguments:
- query_rows: bfloat16 [8, 1024, 2048], P('dp', 'seq'), may hold values from -22 to 22
- key_rows: bfloat16 [8, 1024, 2048], P('dp', 'seq'), may hold values from -7 to 7
- value_rows: bfloat16 [8, 1024, 2048], P('dp', 'seq'), may hold values from -6 to 6
- sink_logit: float32 [16], replicated, may hold values from 6 to 11
- grad_out: bfloat16 [8, 1024, 2048], P('dp', 'seq'), may hold values from -1.6 to 1.6
- pattern: int32 [16, 8, 8], replicated, may hold values from 0 to 7, as said below
Outputs:
- attended: bfloat16 [8, 1024, 2048], P('dp', 'seq')
- grad_query: bfloat16 [8, 1024, 2048], P('dp', 'seq')
- grad_key: bfloat16 [8, 1024, 2048], P('dp', 'seq')
- grad_value: bfloat16 [8, 1024, 2048], P('dp', 'seq')
- grad_sink: float32 [16], replicated
Inputs may be any that keep to these rules, and one draw needn't show every extreme that they name: For each head h and query block b, pattern[h, b] lists 8 distinct key blocks: the three neighbouring blocks b - 1, b, b + 1 (moved inward at the ends of the document), the first and the last block, and blocks drawn at random to fill the row.
All inputs are finite; a program needn't handle non-finite values.
Results may differ from a plain program's by a relative error of at most 0.012.
The roundings to bfloat16 on the way count: a program that leaves them out, or rounds other values in their place, can miss the bound.
Values may be sent and summed in bfloat16 or wider, within the bound.
A program may use at most 64 MiB of HBM per device.

v0:
```python
import jax
import jax.numpy as jnp
from jax import lax
from jax.sharding import PartitionSpec as P

HEAD = 128
BLOCK = 128


tile_group = 4


def tile_scores(queries, key_tiles, scaling):
    return (
        jnp.einsum("gqe,gkbe->gqkb", queries, key_tiles, preferred_element_type=jnp.float32)
        * scaling
    )


def log_totals(scores, sink_value):
    row_top = jnp.maximum(jnp.max(scores, axis=(2, 3)), sink_value)
    summed = jnp.sum(jnp.exp(scores - row_top[:, :, None, None]), axis=(2, 3)) + jnp.exp(
        sink_value - row_top
    )
    return row_top + jnp.log(summed)


def softmax_weights(scores, log_total):
    weights = jnp.exp(scores - log_total[:, :, None, None])
    return (weights, weights.astype(jnp.bfloat16))


def attend(rounded, value_tiles):
    return jnp.einsum(
        "gqkb,gkbe->gqe", rounded, value_tiles, preferred_element_type=jnp.float32
    ).astype(jnp.bfloat16)


def gradients(
    weights,
    rounded,
    attended,
    queries,
    key_tiles,
    value_tiles,
    grad_tile,
    log_total,
    sink_value,
    scaling,
):
    row_dot = jnp.sum(grad_tile.astype(jnp.float32) * attended.astype(jnp.float32), axis=-1)
    grad_weights = jnp.einsum(
        "gqe,gkbe->gqkb", grad_tile, value_tiles, preferred_element_type=jnp.float32
    )
    grad_scores = (weights * (grad_weights - row_dot[:, :, None, None])).astype(jnp.bfloat16)
    grad_query = (
        jnp.einsum("gqkb,gkbe->gqe", grad_scores, key_tiles, preferred_element_type=jnp.float32)
        * scaling
    ).astype(jnp.bfloat16)
    key_part = (
        jnp.einsum("gqkb,gqe->gkbe", grad_scores, queries, preferred_element_type=jnp.float32)
        * scaling
    )
    value_part = jnp.einsum(
        "gqkb,gqe->gkbe", rounded, grad_tile, preferred_element_type=jnp.float32
    )
    sink_part = -jnp.sum(jnp.exp(sink_value - log_total) * row_dot)
    return (grad_query, key_part, value_part, sink_part)


def head_tiles(array_in, head_index):
    row_count = array_in.shape[0]
    picked = lax.dynamic_index_in_dim(array_in, head_index, 1, keepdims=False)
    return picked.reshape(row_count // BLOCK, BLOCK, HEAD)


def put_head(buffer, tiles, head_index):
    return lax.dynamic_update_slice_in_dim(buffer, tiles.reshape(-1, 1, HEAD), head_index, 1)


def group_rows(tiles, group_index):
    return lax.dynamic_slice_in_dim(tiles, group_index * tile_group, tile_group, 0)


def put_group(buffer, tiles, group_index):
    return lax.dynamic_update_slice_in_dim(buffer, tiles, group_index * tile_group, 0)


def put_scalar(buffer, value_in, head_index):
    return lax.dynamic_update_slice_in_dim(buffer, value_in[None], head_index, 0)


def forward_pass(query_heads, key_heads, value_heads, head_links, head_sinks, scaling):
    row_count, local_heads, _ = query_heads.shape
    block_count = row_count // BLOCK

    def forward_one_head(head_index, head_state):
        attended, log_total = head_state
        query_tiles = head_tiles(query_heads, head_index)
        key_all = head_tiles(key_heads, head_index)
        value_all = head_tiles(value_heads, head_index)
        link_rows = lax.dynamic_index_in_dim(head_links, head_index, 0, keepdims=False)
        sink_value = lax.dynamic_index_in_dim(head_sinks, head_index, 0, keepdims=False)

        def forward_one_group(group_index, inner_state):
            out_tiles, total_tiles = inner_state
            chosen = group_rows(link_rows, group_index)
            scores = tile_scores(group_rows(query_tiles, group_index), key_all[chosen], scaling)
            group_total = log_totals(scores, sink_value)
            _, rounded = softmax_weights(scores, group_total)
            result = attend(rounded, value_all[chosen])
            return (
                put_group(out_tiles, result, group_index),
                put_group(total_tiles, group_total, group_index),
            )

        initial = (
            jnp.zeros((block_count, BLOCK, HEAD), jnp.bfloat16),
            jnp.zeros((block_count, BLOCK), jnp.float32),
        )
        out_tiles, total_tiles = lax.fori_loop(
            0, block_count // tile_group, forward_one_group, initial
        )
        return (
            put_head(attended, out_tiles, head_index),
            lax.dynamic_update_slice_in_dim(log_total, total_tiles[None], head_index, 0),
        )

    initial = (
        jnp.zeros((row_count, local_heads, HEAD), jnp.bfloat16),
        jnp.zeros((local_heads, block_count, BLOCK), jnp.float32),
    )
    return lax.fori_loop(0, local_heads, forward_one_head, initial)


def backward_pass(
    query_heads,
    key_heads,
    value_heads,
    grad_heads,
    attended,
    log_total,
    head_links,
    head_sinks,
    scaling,
):
    row_count, local_heads, _ = query_heads.shape
    block_count = row_count // BLOCK

    def backward_one_head(head_index, head_state):
        query_grads, key_grads, value_grads, sink_terms = head_state
        query_tiles = head_tiles(query_heads, head_index)
        key_all = head_tiles(key_heads, head_index)
        value_all = head_tiles(value_heads, head_index)
        grad_tiles = head_tiles(grad_heads, head_index)
        out_tiles = head_tiles(attended, head_index)
        head_total = lax.dynamic_index_in_dim(log_total, head_index, 0, keepdims=False)
        link_rows = lax.dynamic_index_in_dim(head_links, head_index, 0, keepdims=False)
        sink_value = lax.dynamic_index_in_dim(head_sinks, head_index, 0, keepdims=False)

        def backward_one_group(group_index, inner_state):
            query_part_all, key_acc, value_acc, sink_acc = inner_state
            chosen = group_rows(link_rows, group_index)
            queries = group_rows(query_tiles, group_index)
            key_tiles = key_all[chosen]
            value_tiles = value_all[chosen]
            group_total = group_rows(head_total, group_index)
            scores = tile_scores(queries, key_tiles, scaling)
            weights, rounded = softmax_weights(scores, group_total)
            grad_query, key_part, value_part, sink_part = gradients(
                weights,
                rounded,
                group_rows(out_tiles, group_index),
                queries,
                key_tiles,
                value_tiles,
                group_rows(grad_tiles, group_index),
                group_total,
                sink_value,
                scaling,
            )
            flat_links = chosen.reshape(-1)
            key_acc = key_acc.at[flat_links].add(key_part.reshape(-1, BLOCK, HEAD))
            value_acc = value_acc.at[flat_links].add(value_part.reshape(-1, BLOCK, HEAD))
            return (
                put_group(query_part_all, grad_query, group_index),
                key_acc,
                value_acc,
                sink_acc + sink_part,
            )

        initial = (
            jnp.zeros((block_count, BLOCK, HEAD), jnp.bfloat16),
            jnp.zeros((block_count, BLOCK, HEAD), jnp.float32),
            jnp.zeros((block_count, BLOCK, HEAD), jnp.float32),
            jnp.zeros((), jnp.float32),
        )
        query_part_all, key_acc, value_acc, sink_acc = lax.fori_loop(
            0, block_count // tile_group, backward_one_group, initial
        )
        return (
            put_head(query_grads, query_part_all, head_index),
            put_head(key_grads, key_acc.astype(jnp.bfloat16), head_index),
            put_head(value_grads, value_acc.astype(jnp.bfloat16), head_index),
            put_scalar(sink_terms, sink_acc, head_index),
        )

    blank = jnp.zeros((row_count, local_heads, HEAD), jnp.bfloat16)
    initial = (blank, blank, blank, jnp.zeros((local_heads,), jnp.float32))
    return lax.fori_loop(0, local_heads, backward_one_head, initial)


def on_device(query_rows, key_rows, value_rows, sink_logit, grad_out, pattern):
    token_count = query_rows.shape[1]
    head_count = sink_logit.shape[0]
    local_heads = head_count // lax.axis_size("seq")
    first_head = lax.axis_index("seq") * local_heads
    head_links = lax.dynamic_slice_in_dim(pattern, first_head, local_heads, 0)
    head_sinks = lax.dynamic_slice_in_dim(sink_logit, first_head, local_heads, 0)
    scaling = HEAD ** (-0.5)

    def split_heads(array_in):
        return array_in.reshape(token_count, head_count, HEAD)

    def join_heads(array_in):
        return array_in.reshape(1, token_count, head_count * HEAD)

    query_heads, key_heads, value_heads = (
        lax.all_to_all(split_heads(query_rows), "seq", split_axis=1, concat_axis=0, tiled=True),
        lax.all_to_all(split_heads(key_rows), "seq", split_axis=1, concat_axis=0, tiled=True),
        lax.all_to_all(split_heads(value_rows), "seq", split_axis=1, concat_axis=0, tiled=True),
    )
    attended_heads, log_total = forward_pass(
        query_heads, key_heads, value_heads, head_links, head_sinks, scaling
    )
    attended = lax.all_to_all(attended_heads, "seq", split_axis=0, concat_axis=1, tiled=True)
    grad_heads = lax.all_to_all(
        split_heads(grad_out), "seq", split_axis=1, concat_axis=0, tiled=True
    )
    query_grads, key_grads, value_grads, sink_terms = backward_pass(
        query_heads,
        key_heads,
        value_heads,
        grad_heads,
        attended_heads,
        log_total,
        head_links,
        head_sinks,
        scaling,
    )
    grad_query, grad_key, grad_value = (
        lax.all_to_all(query_grads, "seq", split_axis=0, concat_axis=1, tiled=True),
        lax.all_to_all(key_grads, "seq", split_axis=0, concat_axis=1, tiled=True),
        lax.all_to_all(value_grads, "seq", split_axis=0, concat_axis=1, tiled=True),
    )
    spread = lax.dynamic_update_slice_in_dim(
        jnp.zeros((head_count,), jnp.float32), sink_terms, first_head, 0
    )
    summed = lax.psum(spread, ("seq", "dp"))
    grad_sink = summed / lax.axis_size("dp")
    return (
        join_heads(attended),
        join_heads(grad_query),
        join_heads(grad_key),
        join_heads(grad_value),
        grad_sink,
    )


def solution(mesh):
    placed = (
        P("dp", "seq", None),
        P("dp", "seq", None),
        P("dp", "seq", None),
        P(),
        P("dp", "seq", None),
        P(),
    )
    return jax.shard_map(
        on_device,
        mesh=mesh,
        in_specs=placed,
        out_specs=(
            P("dp", "seq", None),
            P("dp", "seq", None),
            P("dp", "seq", None),
            P("dp", "seq", None),
            P(),
        ),
        check_vma=False,
    )
```

profile of v0, /device:TPU:0, one launch (start us, length us, event | category | flops | bytes accessed | tf_op | source)
XLA Modules:
  0.0 460.2 jit_solution(16767909182446267273)
XLA Ops:
  0.7 2.4 copy.51
  3.0 5.2 %all-to-all-start = ((bf16[256,16,128]{0,2,1:T(8,128)(2,1)}), bf16[256,16,128]{0,2,1:T(8,128)(2,1)S(1)}, u32[]{:S(2)}, u32[]{:S(2)}) async-start(bf16[256,16,128]{0,2,1:T(8,128)(2,1)} %bitcast.38), calls=%async_computation | async-start | bytes 2097152 | tf_op jit(solution)/shard_map/all_to_all | solution.py:229
  9.5 12.3 %all-to-all-done = bf16[256,16,128]{0,2,1:T(8,128)(2,1)S(1)} async-done(((bf16[256,16,128]{0,2,1:T(8,128)(2,1)}), bf16[256,16,128]{0,2,1:T(8,128)(2,1)S(1)}, u32[]{:S(2)}, u32[]{:S(2)}) %all-to-all-start) | async-done | bytes 1048608 | tf_op jit(solution)/shard_map/all_to_all | solution.py:229
  21.8 3.5 all-to-all-start.1
  26.7 11.7 %all-to-all-done.1 = bf16[256,16,128]{0,2,1:T(8,128)(2,1)S(1)} async-done(((bf16[256,16,128]{0,2,1:T(8,128)(2,1)}), bf16[256,16,128]{0,2,1:T(8,128)(2,1)S(1)}, u32[]{:S(2)}, u32[]{:S(2)}) %all-to-all-start.1) | async-done | bytes 1048608 | tf_op jit(solution)/shard_map/all_to_all | solution.py:230
  38.4 3.5 all-to-all-start.2
  41.9 2.3 copy.62
  44.2 10.7 %all-to-all-done.2 = bf16[256,16,128]{0,2,1:T(8,128)(2,1)S(1)} async-done(((bf16[256,16,128]{0,2,1:T(8,128)(2,1)}), bf16[256,16,128]{0,2,1:T(8,128)(2,1)S(1)}, u32[]{:S(2)}, u32[]{:S(2)}) %all-to-all-start.2) | async-done | bytes 1048608 | tf_op jit(solution)/shard_map/all_to_all | solution.py:231
  55.0 4.2 all-to-all-start.4
  63.4 8.9 %all-to-all-done.4 = bf16[256,16,128]{0,2,1:T(8,128)(2,1)} async-done(((bf16[256,16,128]{0,2,1:T(8,128)(2,1)}), bf16[256,16,128]{0,2,1:T(8,128)(2,1)}, u32[]{:S(2)}, u32[]{:S(2)}) %all-to-all-start.4) | async-done | bytes 1048608 | tf_op jit(solution)/shard_map/all_to_all | solution.py:237
  75.7 49.4 %while.109 = (s32[]{:T(128)}, bf16[1024,4,128]{2,0,1:T(8,128)(2,1)}, f32[4,8,128]{2,1,0:T(8,128)S(1)}, s32[4,8,8]{2,1,0:T(8,128)S(1)}, bf16[1024,4,128]{2,0,1:T(...) while((s32[]{:T(128)}, bf16[1024,4,128]{2,0,1:T(8,128)(2,1)}, ...), condition=%wide.region_5.6_spmd, body=%wide.region_0.5_spmd.sunk | while | flops 272697952 | bytes 15243110 | solution.py:133
  78.5 8.9 %while.112 = (s32[]{:T(128)}, bf16[8,128,128]{2,1,0:T(8,128)(2,1)S(1)}, f32[8,128]{1,0:T(8,128)S(1)}, bf16[8,128,128]{2,1,0:T(8,128)(2,1)S(1)}, s32[8,8]{1,0:T(8...) while((s32[]{:T(128)}, ...), condition=%wide.region_4.4_spmd, body=%wide.region_1.3_spmd.sunk | while | flops 272697952 | bytes 12870715 | solution.py:121
  90.8 8.9 %while.112 = (s32[]{:T(128)}, bf16[8,128,128]{2,1,0:T(8,128)(2,1)S(1)}, f32[8,128]{1,0:T(8,128)S(1)}, bf16[8,128,128]{2,1,0:T(8,128)(2,1)S(1)}, s32[8,8]{1,0:T(8...) while((s32[]{:T(128)}, ...), condition=%wide.region_4.4_spmd, body=%wide.region_1.3_spmd.sunk | while | flops 272697952 | bytes 12870715 | solution.py:121
  103.2 8.9 %while.112 = (s32[]{:T(128)}, bf16[8,128,128]{2,1,0:T(8,128)(2,1)S(1)}, f32[8,128]{1,0:T(8,128)S(1)}, bf16[8,128,128]{2,1,0:T(8,128)(2,1)S(1)}, s32[8,8]{1,0:T(8...) while((s32[]{:T(128)}, ...), condition=%wide.region_4.4_spmd, body=%wide.region_1.3_spmd.sunk | while | flops 272697952 | bytes 12870715 | solution.py:121
  115.5 8.9 %while.112 = (s32[]{:T(128)}, bf16[8,128,128]{2,1,0:T(8,128)(2,1)S(1)}, f32[8,128]{1,0:T(8,128)S(1)}, bf16[8,128,128]{2,1,0:T(8,128)(2,1)S(1)}, s32[8,8]{1,0:T(8...) while((s32[]{:T(128)}, ...), condition=%wide.region_4.4_spmd, body=%wide.region_1.3_spmd.sunk | while | flops 272697952 | bytes 12870715 | solution.py:121
  125.2 3.0 copy.60
  128.2 4.4 all-to-all-start.3
  136.0 223.2 %while.111 = (s32[]{:T(128)}, bf16[1024,4,128]{2,0,1:T(8,128)(2,1)}, bf16[1024,4,128]{2,0,1:T(8,128)(2,1)}, bf16[1024,4,128]{2,0,1:T(8,128)(2,1)}, f32[4]{0:T(12...) while((s32[]{:T(128)}, bf16[1024,4,128]{2,0,1:T(8,128)(2,1)}, ...), condition=%wide.region_13.14_spmd, body=%wide.region_6.13_spmd.sunk | while | flops 677513408 | bytes 56259804 | solution.py:210
  142.4 46.8 %while.113 = (s32[]{:T(128)}, bf16[8,128,128]{2,1,0:T(8,128)(2,1)}, f32[8,128,128]{2,1,0:T(8,128)S(1)}, f32[8,128,128]{2,1,0:T(8,128)S(1)}, f32[]{:T(128)}, /*in...) while((s32[]{:T(128)}, bf16[8,128,128]{2,1,0:T(8,128)(2,1)}, ...), condition=%wide.region_12.12_spmd, body=%wide.region_7.11_spmd.sunk | while | flops 677251264 | bytes 49172796 | solution.py:198
  150.5 3.0 fusion.69
  153.6 4.7 %scatter_fusion.1 = f32[8,128,128]{2,1,0:T(8,128)S(1)} fusion(f32[8,128,128]{2,1,0:T(8,128)S(1)} %get-tuple-element.1228, s32[32]{0:T(128)S(1)} %fusion.68, f32[32,128,128]{2,1,0:T(8,128)} %bitcast.190), kind=kCustom, calls=%fused_computation.5.clone.1 | custom fusion | flops 524288 | bytes 6291584 | tf_op jit(solution)/shard_map/while/body/eval_jaxpr/while/body/eval_jaxpr/scatter-add | solution.py:184
  158.2 2.8 convolution_multiply_fusion.2
  161.0 4.7 %scatter_fusion = f32[8,128,128]{2,1,0:T(8,128)S(1)} fusion(f32[8,128,128]{2,1,0:T(8,128)S(1)} %get-tuple-element.1227, s32[32]{0:T(128)S(1)} %fusion.68, f32[32,128,128]{2,1,0:T(8,128)} %bitcast.189), kind=kCustom, calls=%fused_computation.4.clone.1 | custom fusion | flops 524288 | bytes 6291584 | tf_op jit(solution)/shard_map/while/body/eval_jaxpr/while/body/eval_jaxpr/scatter-add | solution.py:183
  173.9 3.0 fusion.69
  176.9 4.7 %scatter_fusion.1 = f32[8,128,128]{2,1,0:T(8,128)S(1)} fusion(f32[8,128,128]{2,1,0:T(8,128)S(1)} %get-tuple-element.1228, s32[32]{0:T(128)S(1)} %fusion.68, f32[32,128,128]{2,1,0:T(8,128)} %bitcast.190), kind=kCustom, calls=%fused_computation.5.clone.1 | custom fusion | flops 524288 | bytes 6291584 | tf_op jit(solution)/shard_map/while/body/eval_jaxpr/while/body/eval_jaxpr/scatter-add | solution.py:184
  181.6 2.8 convolution_multiply_fusion.2
  184.4 4.7 %scatter_fusion = f32[8,128,128]{2,1,0:T(8,128)S(1)} fusion(f32[8,128,128]{2,1,0:T(8,128)S(1)} %get-tuple-element.1227, s32[32]{0:T(128)S(1)} %fusion.68, f32[32,128,128]{2,1,0:T(8,128)} %bitcast.189), kind=kCustom, calls=%fused_computation.4.clone.1 | custom fusion | flops 524288 | bytes 6291584 | tf_op jit(solution)/shard_map/while/body/eval_jaxpr/while/body/eval_jaxpr/scatter-add | solution.py:183
  198.2 46.8 %while.113 = (s32[]{:T(128)}, bf16[8,128,128]{2,1,0:T(8,128)(2,1)}, f32[8,128,128]{2,1,0:T(8,128)S(1)}, f32[8,128,128]{2,1,0:T(8,128)S(1)}, f32[]{:T(128)}, /*in...) while((s32[]{:T(128)}, bf16[8,128,128]{2,1,0:T(8,128)(2,1)}, ...), condition=%wide.region_12.12_spmd, body=%wide.region_7.11_spmd.sunk | while | flops 677251264 | bytes 49172796 | solution.py:198
  206.3 3.0 fusion.69
  209.4 4.7 %scatter_fusion.1 = f32[8,128,128]{2,1,0:T(8,128)S(1)} fusion(f32[8,128,128]{2,1,0:T(8,128)S(1)} %get-tuple-element.1228, s32[32]{0:T(128)S(1)} %fusion.68, f32[32,128,128]{2,1,0:T(8,128)} %bitcast.190), kind=kCustom, calls=%fused_computation.5.clone.1 | custom fusion | flops 524288 | bytes 6291584 | tf_op jit(solution)/shard_map/while/body/eval_jaxpr/while/body/eval_jaxpr/scatter-add | solution.py:184
  214.0 2.8 convolution_multiply_fusion.2
  216.8 4.7 %scatter_fusion = f32[8,128,128]{2,1,0:T(8,128)S(1)} fusion(f32[8,128,128]{2,1,0:T(8,128)S(1)} %get-tuple-element.1227, s32[32]{0:T(128)S(1)} %fusion.68, f32[32,128,128]{2,1,0:T(8,128)} %bitcast.189), kind=kCustom, calls=%fused_computation.4.clone.1 | custom fusion | flops 524288 | bytes 6291584 | tf_op jit(solution)/shard_map/while/body/eval_jaxpr/while/body/eval_jaxpr/scatter-add | solution.py:183
  229.7 3.0 fusion.69
  232.8 4.7 %scatter_fusion.1 = f32[8,128,128]{2,1,0:T(8,128)S(1)} fusion(f32[8,128,128]{2,1,0:T(8,128)S(1)} %get-tuple-element.1228, s32[32]{0:T(128)S(1)} %fusion.68, f32[32,128,128]{2,1,0:T(8,128)} %bitcast.190), kind=kCustom, calls=%fused_computation.5.clone.1 | custom fusion | flops 524288 | bytes 6291584 | tf_op jit(solution)/shard_map/while/body/eval_jaxpr/while/body/eval_jaxpr/scatter-add | solution.py:184
  237.4 2.8 convolution_multiply_fusion.2
  240.2 4.7 %scatter_fusion = f32[8,128,128]{2,1,0:T(8,128)S(1)} fusion(f32[8,128,128]{2,1,0:T(8,128)S(1)} %get-tuple-element.1227, s32[32]{0:T(128)S(1)} %fusion.68, f32[32,128,128]{2,1,0:T(8,128)} %bitcast.189), kind=kCustom, calls=%fused_computation.4.clone.1 | custom fusion | flops 524288 | bytes 6291584 | tf_op jit(solution)/shard_map/while/body/eval_jaxpr/while/body/eval_jaxpr/scatter-add | solution.py:183
  254.0 46.8 %while.113 = (s32[]{:T(128)}, bf16[8,128,128]{2,1,0:T(8,128)(2,1)}, f32[8,128,128]{2,1,0:T(8,128)S(1)}, f32[8,128,128]{2,1,0:T(8,128)S(1)}, f32[]{:T(128)}, /*in...) while((s32[]{:T(128)}, bf16[8,128,128]{2,1,0:T(8,128)(2,1)}, ...), condition=%wide.region_12.12_spmd, body=%wide.region_7.11_spmd.sunk | while | flops 677251264 | bytes 49172796 | solution.py:198
  262.1 3.0 fusion.69
  265.1 4.7 %scatter_fusion.1 = f32[8,128,128]{2,1,0:T(8,128)S(1)} fusion(f32[8,128,128]{2,1,0:T(8,128)S(1)} %get-tuple-element.1228, s32[32]{0:T(128)S(1)} %fusion.68, f32[32,128,128]{2,1,0:T(8,128)} %bitcast.190), kind=kCustom, calls=%fused_computation.5.clone.1 | custom fusion | flops 524288 | bytes 6291584 | tf_op jit(solution)/shard_map/while/body/eval_jaxpr/while/body/eval_jaxpr/scatter-add | solution.py:184
  269.8 2.8 convolution_multiply_fusion.2
  272.6 4.7 %scatter_fusion = f32[8,128,128]{2,1,0:T(8,128)S(1)} fusion(f32[8,128,128]{2,1,0:T(8,128)S(1)} %get-tuple-element.1227, s32[32]{0:T(128)S(1)} %fusion.68, f32[32,128,128]{2,1,0:T(8,128)} %bitcast.189), kind=kCustom, calls=%fused_computation.4.clone.1 | custom fusion | flops 524288 | bytes 6291584 | tf_op jit(solution)/shard_map/while/body/eval_jaxpr/while/body/eval_jaxpr/scatter-add | solution.py:183
  285.5 3.0 fusion.69
  288.5 4.7 %scatter_fusion.1 = f32[8,128,128]{2,1,0:T(8,128)S(1)} fusion(f32[8,128,128]{2,1,0:T(8,128)S(1)} %get-tuple-element.1228, s32[32]{0:T(128)S(1)} %fusion.68, f32[32,128,128]{2,1,0:T(8,128)} %bitcast.190), kind=kCustom, calls=%fused_computation.5.clone.1 | custom fusion | flops 524288 | bytes 6291584 | tf_op jit(solution)/shard_map/while/body/eval_jaxpr/while/body/eval_jaxpr/scatter-add | solution.py:184
  293.2 2.8 convolution_multiply_fusion.2
  296.0 4.7 %scatter_fusion = f32[8,128,128]{2,1,0:T(8,128)S(1)} fusion(f32[8,128,128]{2,1,0:T(8,128)S(1)} %get-tuple-element.1227, s32[32]{0:T(128)S(1)} %fusion.68, f32[32,128,128]{2,1,0:T(8,128)} %bitcast.189), kind=kCustom, calls=%fused_computation.4.clone.1 | custom fusion | flops 524288 | bytes 6291584 | tf_op jit(solution)/shard_map/while/body/eval_jaxpr/while/body/eval_jaxpr/scatter-add | solution.py:183
  309.8 46.8 %while.113 = (s32[]{:T(128)}, bf16[8,128,128]{2,1,0:T(8,128)(2,1)}, f32[8,128,128]{2,1,0:T(8,128)S(1)}, f32[8,128,128]{2,1,0:T(8,128)S(1)}, f32[]{:T(128)}, /*in...) while((s32[]{:T(128)}, bf16[8,128,128]{2,1,0:T(8,128)(2,1)}, ...), condition=%wide.region_12.12_spmd, body=%wide.region_7.11_spmd.sunk | while | flops 677251264 | bytes 49172796 | solution.py:198
  317.9 3.0 fusion.69
  320.9 4.7 %scatter_fusion.1 = f32[8,128,128]{2,1,0:T(8,128)S(1)} fusion(f32[8,128,128]{2,1,0:T(8,128)S(1)} %get-tuple-element.1228, s32[32]{0:T(128)S(1)} %fusion.68, f32[32,128,128]{2,1,0:T(8,128)} %bitcast.190), kind=kCustom, calls=%fused_computation.5.clone.1 | custom fusion | flops 524288 | bytes 6291584 | tf_op jit(solution)/shard_map/while/body/eval_jaxpr/while/body/eval_jaxpr/scatter-add | solution.py:184
  325.6 2.8 convolution_multiply_fusion.2
  328.4 4.7 %scatter_fusion = f32[8,128,128]{2,1,0:T(8,128)S(1)} fusion(f32[8,128,128]{2,1,0:T(8,128)S(1)} %get-tuple-element.1227, s32[32]{0:T(128)S(1)} %fusion.68, f32[32,128,128]{2,1,0:T(8,128)} %bitcast.189), kind=kCustom, calls=%fused_computation.4.clone.1 | custom fusion | flops 524288 | bytes 6291584 | tf_op jit(solution)/shard_map/while/body/eval_jaxpr/while/body/eval_jaxpr/scatter-add | solution.py:183
  341.3 3.0 fusion.69
  344.3 4.7 %scatter_fusion.1 = f32[8,128,128]{2,1,0:T(8,128)S(1)} fusion(f32[8,128,128]{2,1,0:T(8,128)S(1)} %get-tuple-element.1228, s32[32]{0:T(128)S(1)} %fusion.68, f32[32,128,128]{2,1,0:T(8,128)} %bitcast.190), kind=kCustom, calls=%fused_computation.5.clone.1 | custom fusion | flops 524288 | bytes 6291584 | tf_op jit(solution)/shard_map/while/body/eval_jaxpr/while/body/eval_jaxpr/scatter-add | solution.py:184
  349.0 2.8 convolution_multiply_fusion.2
  351.8 4.7 %scatter_fusion = f32[8,128,128]{2,1,0:T(8,128)S(1)} fusion(f32[8,128,128]{2,1,0:T(8,128)S(1)} %get-tuple-element.1227, s32[32]{0:T(128)S(1)} %fusion.68, f32[32,128,128]{2,1,0:T(8,128)} %bitcast.189), kind=kCustom, calls=%fused_computation.4.clone.1 | custom fusion | flops 524288 | bytes 6291584 | tf_op jit(solution)/shard_map/while/body/eval_jaxpr/while/body/eval_jaxpr/scatter-add | solution.py:183
  359.2 3.1 copy.65
  362.3 4.0 all-to-all-start.5
  368.1 10.8 %all-to-all-done.5 = bf16[1024,4,128]{2,1,0:T(4,128)(2,1)S(1)} async-done(((bf16[1024,4,128]{2,1,0:T(4,128)(2,1)}), bf16[1024,4,128]{2,1,0:T(4,128)(2,1)S(1)}, u32[]{:S(2)}, u32[]{:S(2)}) %all-to-all-start.5) | async-done | bytes 1048608 | tf_op jit(solution)/shard_map/all_to_all | solution.py:252
  378.9 3.5 all-to-all-start.6
  384.2 11.2 %all-to-all-done.6 = bf16[1024,4,128]{2,1,0:T(4,128)(2,1)S(1)} async-done(((bf16[1024,4,128]{2,1,0:T(4,128)(2,1)}), bf16[1024,4,128]{2,1,0:T(4,128)(2,1)S(1)}, u32[]{:S(2)}, u32[]{:S(2)}) %all-to-all-start.6) | async-done | bytes 1048608 | tf_op jit(solution)/shard_map/all_to_all | solution.py:253
  395.5 3.5 all-to-all-start.7
  399.2 47.4 %psum.7 = f32[16]{0:T(128)S(1)} all-reduce(f32[16]{0:T(128)S(1)} %dynamic_update_slice.66), channel_id=1, replica_groups=mesh['seq'=4,'dp'=8] {'seq','dp'}, use_global_device_ids=true, to_apply=%region_14.15 | all-reduce | flops 16 | bytes 128 | tf_op jit(solution)/shard_map/psum | solution.py:259
  447.1 2.6 copy.61
  449.7 2.6 reshape.201
  453.6 2.6 reshape.203
  (487 shorter events, 167.3 us)
Async XLA Ops:
  0.6 58.7 %copy-start = (s32[16,8,8]{0,2,1:T(8,128)S(1)}, s32[16,8,8]{0,2,1:T(8,128)}, u32[]{:S(2)}) copy-start(s32[16,8,8]{0,2,1:T(8,128)} %param.19) | copy-start | bytes 12292
  0.6 7.5 %copy-start.14 = (bf16[1,256,2048]{2,1,0:T(8,128)(2,1)S(1)}, bf16[1,256,2048]{2,1,0:T(8,128)(2,1)}, u32[]{:S(2)}) copy-start(bf16[1,256,2048]{2,1,0:T(8,128)(2,1)} %param.15) | copy-start | bytes 3145732
  3.0 18.8 %all-to-all-start = ((bf16[256,16,128]{0,2,1:T(8,128)(2,1)}), bf16[256,16,128]{0,2,1:T(8,128)(2,1)S(1)}, u32[]{:S(2)}, u32[]{:S(2)}) async-start(bf16[256,16,128]{0,2,1:T(8,128)(2,1)} %bitcast.38), calls=%async_computation | async-start | bytes 2097152 | tf_op jit(solution)/shard_map/all_to_all | solution.py:229
  8.2 17.2 %copy-start.15 = (bf16[1,256,2048]{2,1,0:T(8,128)(2,1)S(1)}, bf16[1,256,2048]{2,1,0:T(8,128)(2,1)}, u32[]{:S(2)}) copy-start(bf16[1,256,2048]{2,1,0:T(8,128)(2,1)} %param.16) | copy-start | bytes 3145732
  21.8 16.6 %all-to-all-start.1 = ((bf16[256,16,128]{0,2,1:T(8,128)(2,1)}), bf16[256,16,128]{0,2,1:T(8,128)(2,1)S(1)}, u32[]{:S(2)}, u32[]{:S(2)}) async-start(bf16[256,16,128]{0,2,1:T(8,128)(2,1)} %bitcast.43), calls=%async_computation.1 | async-start | bytes 2097152 | tf_op jit(solution)/shard_map/all_to_all | solution.py:230
  38.4 16.6 %all-to-all-start.2 = ((bf16[256,16,128]{0,2,1:T(8,128)(2,1)}), bf16[256,16,128]{0,2,1:T(8,128)(2,1)S(1)}, u32[]{:S(2)}, u32[]{:S(2)}) async-start(bf16[256,16,128]{0,2,1:T(8,128)(2,1)} %bitcast.213), calls=%async_computation.2 | async-start | bytes 2097152 | tf_op jit(solution)/shard_map/all_to_all | solution.py:231
  41.9 17.3 %copy-start.16 = (f32[16]{0:T(128)S(1)}, f32[16]{0:T(128)}, u32[]{:S(2)}) copy-start(f32[16]{0:T(128)} %param.17) | copy-start | bytes 196
  55.0 17.4 %all-to-all-start.4 = ((bf16[256,16,128]{0,2,1:T(8,128)(2,1)}), bf16[256,16,128]{0,2,1:T(8,128)(2,1)}, u32[]{:S(2)}, u32[]{:S(2)}) async-start(bf16[256,16,128]{0,2,1:T(8,128)(2,1)} %bitcast.210), calls=%async_computation.4 | async-start | bytes 2097152 | tf_op jit(solution)/shard_map/all_to_all | solution.py:237
  128.2 234.1 %all-to-all-start.3 = ((bf16[1024,4,128]{2,1,0:T(4,128)(2,1)}), bf16[1024,4,128]{2,1,0:T(4,128)(2,1)}, u32[]{:S(2)}, u32[]{:S(2)}) async-start(bf16[1024,4,128]{2,1,0:T(4,128)(2,1)} %copy.60), calls=%async_computation.3 | async-start | bytes 2097152 | tf_op jit(solution)/shard_map/all_to_all | solution.py:236
  142.4 4.7 %copy-start.1 = (bf16[8,128,128]{2,1,0:T(8,128)(2,1)}, bf16[8,128,128]{2,1,0:T(8,128)(2,1)S(1)}, u32[]{:S(2)}) copy-start(bf16[8,128,128]{2,1,0:T(8,128)(2,1)S(1)} %get-tuple-element.1249) | copy-start | bytes 786436 | tf_op jit(solution)/shard_map/while/body/eval_jaxpr/while
  142.4 4.8 %copy-start.4 = (bf16[8,128,128]{2,1,0:T(8,128)(2,1)}, bf16[8,128,128]{2,1,0:T(8,128)(2,1)S(1)}, u32[]{:S(2)}) copy-start(bf16[8,128,128]{2,1,0:T(8,128)(2,1)S(1)} %get-tuple-element.1251) | copy-start | bytes 786436 | tf_op jit(solution)/shard_map/while/body/eval_jaxpr/while
  142.4 4.8 %copy-start.8 = (bf16[8,128,128]{2,1,0:T(8,128)(2,1)}, bf16[8,128,128]{2,1,0:T(8,128)(2,1)S(1)}, u32[]{:S(2)}) copy-start(bf16[8,128,128]{2,1,0:T(8,128)(2,1)S(1)} %get-tuple-element.1253) | copy-start | bytes 786436 | tf_op jit(solution)/shard_map/while/body/eval_jaxpr/while
  142.4 4.8 %copy-start.6 = (bf16[8,128,128]{2,1,0:T(8,128)(2,1)}, bf16[8,128,128]{2,1,0:T(8,128)(2,1)S(1)}, u32[]{:S(2)}) copy-start(bf16[8,128,128]{2,1,0:T(8,128)(2,1)S(1)} %get-tuple-element.1247) | copy-start | bytes 786436 | tf_op jit(solution)/shard_map/while/body/eval_jaxpr/while
  161.0 4.7 %copy-start.5 = (bf16[8,128,128]{2,1,0:T(8,128)(2,1)S(1)}, bf16[8,128,128]{2,1,0:T(8,128)(2,1)}, u32[]{:S(2)}) copy-start(bf16[8,128,128]{2,1,0:T(8,128)(2,1)} %copy-done.4) | copy-start | bytes 786436 | tf_op jit(solution)/shard_map/while/body/eval_jaxpr/while
  161.0 4.7 %copy-start.7 = (bf16[8,128,128]{2,1,0:T(8,128)(2,1)S(1)}, bf16[8,128,128]{2,1,0:T(8,128)(2,1)}, u32[]{:S(2)}) copy-start(bf16[8,128,128]{2,1,0:T(8,128)(2,1)} %copy-done.6) | copy-start | bytes 786436 | tf_op jit(solution)/shard_map/while/body/eval_jaxpr/while
  161.0 4.7 %copy-start.9 = (bf16[8,128,128]{2,1,0:T(8,128)(2,1)S(1)}, bf16[8,128,128]{2,1,0:T(8,128)(2,1)}, u32[]{:S(2)}) copy-start(bf16[8,128,128]{2,1,0:T(8,128)(2,1)} %copy-done.8) | copy-start | bytes 786436 | tf_op jit(solution)/shard_map/while/body/eval_jaxpr/while
  165.7 4.8 %copy-start.1 = (bf16[8,128,128]{2,1,0:T(8,128)(2,1)}, bf16[8,128,128]{2,1,0:T(8,128)(2,1)S(1)}, u32[]{:S(2)}) copy-start(bf16[8,128,128]{2,1,0:T(8,128)(2,1)S(1)} %get-tuple-element.1249) | copy-start | bytes 786436 | tf_op jit(solution)/shard_map/while/body/eval_jaxpr/while
  165.7 4.8 %copy-start.4 = (bf16[8,128,128]{2,1,0:T(8,128)(2,1)}, bf16[8,128,128]{2,1,0:T(8,128)(2,1)S(1)}, u32[]{:S(2)}) copy-start(bf16[8,128,128]{2,1,0:T(8,128)(2,1)S(1)} %get-tuple-element.1251) | copy-start | bytes 786436 | tf_op jit(solution)/shard_map/while/body/eval_jaxpr/while
  165.8 4.8 %copy-start.8 = (bf16[8,128,128]{2,1,0:T(8,128)(2,1)}, bf16[8,128,128]{2,1,0:T(8,128)(2,1)S(1)}, u32[]{:S(2)}) copy-start(bf16[8,128,128]{2,1,0:T(8,128)(2,1)S(1)} %get-tuple-element.1253) | copy-start | bytes 786436 | tf_op jit(solution)/shard_map/while/body/eval_jaxpr/while
  165.8 4.8 %copy-start.6 = (bf16[8,128,128]{2,1,0:T(8,128)(2,1)}, bf16[8,128,128]{2,1,0:T(8,128)(2,1)S(1)}, u32[]{:S(2)}) copy-start(bf16[8,128,128]{2,1,0:T(8,128)(2,1)S(1)} %get-tuple-element.1247) | copy-start | bytes 786436 | tf_op jit(solution)/shard_map/while/body/eval_jaxpr/while
  184.4 4.7 %copy-start.5 = (bf16[8,128,128]{2,1,0:T(8,128)(2,1)S(1)}, bf16[8,128,128]{2,1,0:T(8,128)(2,1)}, u32[]{:S(2)}) copy-start(bf16[8,128,128]{2,1,0:T(8,128)(2,1)} %copy-done.4) | copy-start | bytes 786436 | tf_op jit(solution)/shard_map/while/body/eval_jaxpr/while
  184.4 4.7 %copy-start.7 = (bf16[8,128,128]{2,1,0:T(8,128)(2,1)S(1)}, bf16[8,128,128]{2,1,0:T(8,128)(2,1)}, u32[]{:S(2)}) copy-start(bf16[8,128,128]{2,1,0:T(8,128)(2,1)} %copy-done.6) | copy-start | bytes 786436 | tf_op jit(solution)/shard_map/while/body/eval_jaxpr/while
  184.4 4.7 %copy-start.9 = (bf16[8,128,128]{2,1,0:T(8,128)(2,1)S(1)}, bf16[8,128,128]{2,1,0:T(8,128)(2,1)}, u32[]{:S(2)}) copy-start(bf16[8,128,128]{2,1,0:T(8,128)(2,1)} %copy-done.8) | copy-start | bytes 786436 | tf_op jit(solution)/shard_map/while/body/eval_jaxpr/while
  198.2 4.7 %copy-start.1 = (bf16[8,128,128]{2,1,0:T(8,128)(2,1)}, bf16[8,128,128]{2,1,0:T(8,128)(2,1)S(1)}, u32[]{:S(2)}) copy-start(bf16[8,128,128]{2,1,0:T(8,128)(2,1)S(1)} %get-tuple-element.1249) | copy-start | bytes 786436 | tf_op jit(solution)/shard_map/while/body/eval_jaxpr/while
  198.2 4.8 %copy-start.4 = (bf16[8,128,128]{2,1,0:T(8,128)(2,1)}, bf16[8,128,128]{2,1,0:T(8,128)(2,1)S(1)}, u32[]{:S(2)}) copy-start(bf16[8,128,128]{2,1,0:T(8,128)(2,1)S(1)} %get-tuple-element.1251) | copy-start | bytes 786436 | tf_op jit(solution)/shard_map/while/body/eval_jaxpr/while
  198.2 4.8 %copy-start.8 = (bf16[8,128,128]{2,1,0:T(8,128)(2,1)}, bf16[8,128,128]{2,1,0:T(8,128)(2,1)S(1)}, u32[]{:S(2)}) copy-start(bf16[8,128,128]{2,1,0:T(8,128)(2,1)S(1)} %get-tuple-element.1253) | copy-start | bytes 786436 | tf_op jit(solution)/shard_map/while/body/eval_jaxpr/while
  198.2 4.8 %copy-start.6 = (bf16[8,128,128]{2,1,0:T(8,128)(2,1)}, bf16[8,128,128]{2,1,0:T(8,128)(2,1)S(1)}, u32[]{:S(2)}) copy-start(bf16[8,128,128]{2,1,0:T(8,128)(2,1)S(1)} %get-tuple-element.1247) | copy-start | bytes 786436 | tf_op jit(solution)/shard_map/while/body/eval_jaxpr/while
  216.8 4.7 %copy-start.7 = (bf16[8,128,128]{2,1,0:T(8,128)(2,1)S(1)}, bf16[8,128,128]{2,1,0:T(8,128)(2,1)}, u32[]{:S(2)}) copy-start(bf16[8,128,128]{2,1,0:T(8,128)(2,1)} %copy-done.6) | copy-start | bytes 786436 | tf_op jit(solution)/shard_map/while/body/eval_jaxpr/while
  216.8 4.7 %copy-start.9 = (bf16[8,128,128]{2,1,0:T(8,128)(2,1)S(1)}, bf16[8,128,128]{2,1,0:T(8,128)(2,1)}, u32[]{:S(2)}) copy-start(bf16[8,128,128]{2,1,0:T(8,128)(2,1)} %copy-done.8) | copy-start | bytes 786436 | tf_op jit(solution)/shard_map/while/body/eval_jaxpr/while
  221.5 4.8 %copy-start.1 = (bf16[8,128,128]{2,1,0:T(8,128)(2,1)}, bf16[8,128,128]{2,1,0:T(8,128)(2,1)S(1)}, u32[]{:S(2)}) copy-start(bf16[8,128,128]{2,1,0:T(8,128)(2,1)S(1)} %get-tuple-element.1249) | copy-start | bytes 786436 | tf_op jit(solution)/shard_map/while/body/eval_jaxpr/while
  221.6 4.8 %copy-start.4 = (bf16[8,128,128]{2,1,0:T(8,128)(2,1)}, bf16[8,128,128]{2,1,0:T(8,128)(2,1)S(1)}, u32[]{:S(2)}) copy-start(bf16[8,128,128]{2,1,0:T(8,128)(2,1)S(1)} %get-tuple-element.1251) | copy-start | bytes 786436 | tf_op jit(solution)/shard_map/while/body/eval_jaxpr/while
  221.6 4.8 %copy-start.8 = (bf16[8,128,128]{2,1,0:T(8,128)(2,1)}, bf16[8,128,128]{2,1,0:T(8,128)(2,1)S(1)}, u32[]{:S(2)}) copy-start(bf16[8,128,128]{2,1,0:T(8,128)(2,1)S(1)} %get-tuple-element.1253) | copy-start | bytes 786436 | tf_op jit(solution)/shard_map/while/body/eval_jaxpr/while
  221.6 4.8 %copy-start.6 = (bf16[8,128,128]{2,1,0:T(8,128)(2,1)}, bf16[8,128,128]{2,1,0:T(8,128)(2,1)S(1)}, u32[]{:S(2)}) copy-start(bf16[8,128,128]{2,1,0:T(8,128)(2,1)S(1)} %get-tuple-element.1247) | copy-start | bytes 786436 | tf_op jit(solution)/shard_map/while/body/eval_jaxpr/while
  240.2 4.7 %copy-start.7 = (bf16[8,128,128]{2,1,0:T(8,128)(2,1)S(1)}, bf16[8,128,128]{2,1,0:T(8,128)(2,1)}, u32[]{:S(2)}) copy-start(bf16[8,128,128]{2,1,0:T(8,128)(2,1)} %copy-done.6) | copy-start | bytes 786436 | tf_op jit(solution)/shard_map/while/body/eval_jaxpr/while
  240.2 4.7 %copy-start.9 = (bf16[8,128,128]{2,1,0:T(8,128)(2,1)S(1)}, bf16[8,128,128]{2,1,0:T(8,128)(2,1)}, u32[]{:S(2)}) copy-start(bf16[8,128,128]{2,1,0:T(8,128)(2,1)} %copy-done.8) | copy-start | bytes 786436 | tf_op jit(solution)/shard_map/while/body/eval_jaxpr/while
  254.0 4.7 %copy-start.1 = (bf16[8,128,128]{2,1,0:T(8,128)(2,1)}, bf16[8,128,128]{2,1,0:T(8,128)(2,1)S(1)}, u32[]{:S(2)}) copy-start(bf16[8,128,128]{2,1,0:T(8,128)(2,1)S(1)} %get-tuple-element.1249) | copy-start | bytes 786436 | tf_op jit(solution)/shard_map/while/body/eval_jaxpr/while
  254.0 4.8 %copy-start.4 = (bf16[8,128,128]{2,1,0:T(8,128)(2,1)}, bf16[8,128,128]{2,1,0:T(8,128)(2,1)S(1)}, u32[]{:S(2)}) copy-start(bf16[8,128,128]{2,1,0:T(8,128)(2,1)S(1)} %get-tuple-element.1251) | copy-start | bytes 786436 | tf_op jit(solution)/shard_map/while/body/eval_jaxpr/while
  254.0 4.8 %copy-start.8 = (bf16[8,128,128]{2,1,0:T(8,128)(2,1)}, bf16[8,128,128]{2,1,0:T(8,128)(2,1)S(1)}, u32[]{:S(2)}) copy-start(bf16[8,128,128]{2,1,0:T(8,128)(2,1)S(1)} %get-tuple-element.1253) | copy-start | bytes 786436 | tf_op jit(solution)/shard_map/while/body/eval_jaxpr/while
  254.0 4.8 %copy-start.6 = (bf16[8,128,128]{2,1,0:T(8,128)(2,1)}, bf16[8,128,128]{2,1,0:T(8,128)(2,1)S(1)}, u32[]{:S(2)}) copy-start(bf16[8,128,128]{2,1,0:T(8,128)(2,1)S(1)} %get-tuple-element.1247) | copy-start | bytes 786436 | tf_op jit(solution)/shard_map/while/body/eval_jaxpr/while
  272.6 4.7 %copy-start.7 = (bf16[8,128,128]{2,1,0:T(8,128)(2,1)S(1)}, bf16[8,128,128]{2,1,0:T(8,128)(2,1)}, u32[]{:S(2)}) copy-start(bf16[8,128,128]{2,1,0:T(8,128)(2,1)} %copy-done.6) | copy-start | bytes 786436 | tf_op jit(solution)/shard_map/while/body/eval_jaxpr/while
  272.6 4.7 %copy-start.9 = (bf16[8,128,128]{2,1,0:T(8,128)(2,1)S(1)}, bf16[8,128,128]{2,1,0:T(8,128)(2,1)}, u32[]{:S(2)}) copy-start(bf16[8,128,128]{2,1,0:T(8,128)(2,1)} %copy-done.8) | copy-start | bytes 786436 | tf_op jit(solution)/shard_map/while/body/eval_jaxpr/while
  277.3 4.8 %copy-start.1 = (bf16[8,128,128]{2,1,0:T(8,128)(2,1)}, bf16[8,128,128]{2,1,0:T(8,128)(2,1)S(1)}, u32[]{:S(2)}) copy-start(bf16[8,128,128]{2,1,0:T(8,128)(2,1)S(1)} %get-tuple-element.1249) | copy-start | bytes 786436 | tf_op jit(solution)/shard_map/while/body/eval_jaxpr/while
  277.3 4.8 %copy-start.4 = (bf16[8,128,128]{2,1,0:T(8,128)(2,1)}, bf16[8,128,128]{2,1,0:T(8,128)(2,1)S(1)}, u32[]{:S(2)}) copy-start(bf16[8,128,128]{2,1,0:T(8,128)(2,1)S(1)} %get-tuple-element.1251) | copy-start | bytes 786436 | tf_op jit(solution)/shard_map/while/body/eval_jaxpr/while
  277.4 4.8 %copy-start.8 = (bf16[8,128,128]{2,1,0:T(8,128)(2,1)}, bf16[8,128,128]{2,1,0:T(8,128)(2,1)S(1)}, u32[]{:S(2)}) copy-start(bf16[8,128,128]{2,1,0:T(8,128)(2,1)S(1)} %get-tuple-element.1253) | copy-start | bytes 786436 | tf_op jit(solution)/shard_map/while/body/eval_jaxpr/while
  277.4 4.8 %copy-start.6 = (bf16[8,128,128]{2,1,0:T(8,128)(2,1)}, bf16[8,128,128]{2,1,0:T(8,128)(2,1)S(1)}, u32[]{:S(2)}) copy-start(bf16[8,128,128]{2,1,0:T(8,128)(2,1)S(1)} %get-tuple-element.1247) | copy-start | bytes 786436 | tf_op jit(solution)/shard_map/while/body/eval_jaxpr/while
  296.0 4.7 %copy-start.7 = (bf16[8,128,128]{2,1,0:T(8,128)(2,1)S(1)}, bf16[8,128,128]{2,1,0:T(8,128)(2,1)}, u32[]{:S(2)}) copy-start(bf16[8,128,128]{2,1,0:T(8,128)(2,1)} %copy-done.6) | copy-start | bytes 786436 | tf_op jit(solution)/shard_map/while/body/eval_jaxpr/while
  296.0 4.7 %copy-start.9 = (bf16[8,128,128]{2,1,0:T(8,128)(2,1)S(1)}, bf16[8,128,128]{2,1,0:T(8,128)(2,1)}, u32[]{:S(2)}) copy-start(bf16[8,128,128]{2,1,0:T(8,128)(2,1)} %copy-done.8) | copy-start | bytes 786436 | tf_op jit(solution)/shard_map/while/body/eval_jaxpr/while
  309.8 4.7 %copy-start.1 = (bf16[8,128,128]{2,1,0:T(8,128)(2,1)}, bf16[8,128,128]{2,1,0:T(8,128)(2,1)S(1)}, u32[]{:S(2)}) copy-start(bf16[8,128,128]{2,1,0:T(8,128)(2,1)S(1)} %get-tuple-element.1249) | copy-start | bytes 786436 | tf_op jit(solution)/shard_map/while/body/eval_jaxpr/while
  309.8 4.8 %copy-start.4 = (bf16[8,128,128]{2,1,0:T(8,128)(2,1)}, bf16[8,128,128]{2,1,0:T(8,128)(2,1)S(1)}, u32[]{:S(2)}) copy-start(bf16[8,128,128]{2,1,0:T(8,128)(2,1)S(1)} %get-tuple-element.1251) | copy-start | bytes 786436 | tf_op jit(solution)/shard_map/while/body/eval_jaxpr/while
  309.8 4.8 %copy-start.8 = (bf16[8,128,128]{2,1,0:T(8,128)(2,1)}, bf16[8,128,128]{2,1,0:T(8,128)(2,1)S(1)}, u32[]{:S(2)}) copy-start(bf16[8,128,128]{2,1,0:T(8,128)(2,1)S(1)} %get-tuple-element.1253) | copy-start | bytes 786436 | tf_op jit(solution)/shard_map/while/body/eval_jaxpr/while
  309.8 4.8 %copy-start.6 = (bf16[8,128,128]{2,1,0:T(8,128)(2,1)}, bf16[8,128,128]{2,1,0:T(8,128)(2,1)S(1)}, u32[]{:S(2)}) copy-start(bf16[8,128,128]{2,1,0:T(8,128)(2,1)S(1)} %get-tuple-element.1247) | copy-start | bytes 786436 | tf_op jit(solution)/shard_map/while/body/eval_jaxpr/while
  328.4 4.7 %copy-start.7 = (bf16[8,128,128]{2,1,0:T(8,128)(2,1)S(1)}, bf16[8,128,128]{2,1,0:T(8,128)(2,1)}, u32[]{:S(2)}) copy-start(bf16[8,128,128]{2,1,0:T(8,128)(2,1)} %copy-done.6) | copy-start | bytes 786436 | tf_op jit(solution)/shard_map/while/body/eval_jaxpr/while
  328.4 4.7 %copy-start.9 = (bf16[8,128,128]{2,1,0:T(8,128)(2,1)S(1)}, bf16[8,128,128]{2,1,0:T(8,128)(2,1)}, u32[]{:S(2)}) copy-start(bf16[8,128,128]{2,1,0:T(8,128)(2,1)} %copy-done.8) | copy-start | bytes 786436 | tf_op jit(solution)/shard_map/while/body/eval_jaxpr/while
  333.1 4.8 %copy-start.1 = (bf16[8,128,128]{2,1,0:T(8,128)(2,1)}, bf16[8,128,128]{2,1,0:T(8,128)(2,1)S(1)}, u32[]{:S(2)}) copy-start(bf16[8,128,128]{2,1,0:T(8,128)(2,1)S(1)} %get-tuple-element.1249) | copy-start | bytes 786436 | tf_op jit(solution)/shard_map/while/body/eval_jaxpr/while
  333.1 4.8 %copy-start.4 = (bf16[8,128,128]{2,1,0:T(8,128)(2,1)}, bf16[8,128,128]{2,1,0:T(8,128)(2,1)S(1)}, u32[]{:S(2)}) copy-start(bf16[8,128,128]{2,1,0:T(8,128)(2,1)S(1)} %get-tuple-element.1251) | copy-start | bytes 786436 | tf_op jit(solution)/shard_map/while/body/eval_jaxpr/while
  333.1 4.8 %copy-start.8 = (bf16[8,128,128]{2,1,0:T(8,128)(2,1)}, bf16[8,128,128]{2,1,0:T(8,128)(2,1)S(1)}, u32[]{:S(2)}) copy-start(bf16[8,128,128]{2,1,0:T(8,128)(2,1)S(1)} %get-tuple-element.1253) | copy-start | bytes 786436 | tf_op jit(solution)/shard_map/while/body/eval_jaxpr/while
  333.2 4.8 %copy-start.6 = (bf16[8,128,128]{2,1,0:T(8,128)(2,1)}, bf16[8,128,128]{2,1,0:T(8,128)(2,1)S(1)}, u32[]{:S(2)}) copy-start(bf16[8,128,128]{2,1,0:T(8,128)(2,1)S(1)} %get-tuple-element.1247) | copy-start | bytes 786436 | tf_op jit(solution)/shard_map/while/body/eval_jaxpr/while
  351.8 4.7 %copy-start.7 = (bf16[8,128,128]{2,1,0:T(8,128)(2,1)S(1)}, bf16[8,128,128]{2,1,0:T(8,128)(2,1)}, u32[]{:S(2)}) copy-start(bf16[8,128,128]{2,1,0:T(8,128)(2,1)} %copy-done.6) | copy-start | bytes 786436 | tf_op jit(solution)/shard_map/while/body/eval_jaxpr/while
  351.8 4.7 %copy-start.9 = (bf16[8,128,128]{2,1,0:T(8,128)(2,1)S(1)}, bf16[8,128,128]{2,1,0:T(8,128)(2,1)}, u32[]{:S(2)}) copy-start(bf16[8,128,128]{2,1,0:T(8,128)(2,1)} %copy-done.8) | copy-start | bytes 786436 | tf_op jit(solution)/shard_map/while/body/eval_jaxpr/while
  359.2 7.1 %copy-start.13 = (bf16[1024,4,128]{2,0,1:T(8,128)(2,1)S(1)}, bf16[1024,4,128]{2,0,1:T(8,128)(2,1)}, u32[]{:S(2)}) copy-start(bf16[1024,4,128]{2,0,1:T(8,128)(2,1)} %get-tuple-element.772) | copy-start | bytes 3145732
  362.3 16.6 %all-to-all-start.5 = ((bf16[1024,4,128]{2,1,0:T(4,128)(2,1)}), bf16[1024,4,128]{2,1,0:T(4,128)(2,1)S(1)}, u32[]{:S(2)}, u32[]{:S(2)}) async-start(bf16[1024,4,128]{2,1,0:T(4,128)(2,1)} %copy.65), calls=%async_computation.5 | async-start | bytes 2097152 | tf_op jit(solution)/shard_map/all_to_all | solution.py:252
  366.3 16.1 %copy-start.12 = (bf16[1024,4,128]{2,0,1:T(8,128)(2,1)S(1)}, bf16[1024,4,128]{2,0,1:T(8,128)(2,1)}, u32[]{:S(2)}) copy-start(bf16[1024,4,128]{2,0,1:T(8,128)(2,1)} %get-tuple-element.773) | copy-start | bytes 3145732
  378.9 16.6 %all-to-all-start.6 = ((bf16[1024,4,128]{2,1,0:T(4,128)(2,1)}), bf16[1024,4,128]{2,1,0:T(4,128)(2,1)S(1)}, u32[]{:S(2)}, u32[]{:S(2)}) async-start(bf16[1024,4,128]{2,1,0:T(4,128)(2,1)} %copy.67), calls=%async_computation.6 | async-start | bytes 2097152 | tf_op jit(solution)/shard_map/all_to_all | solution.py:253
  395.5 62.7 %all-to-all-start.7 = ((bf16[1024,4,128]{2,1,0:T(4,128)(2,1)}), bf16[1024,4,128]{2,1,0:T(4,128)(2,1)S(1)}, u32[]{:S(2)}, u32[]{:S(2)}) async-start(bf16[1024,4,128]{2,1,0:T(4,128)(2,1)} %copy.69), calls=%async_computation.7 | async-start | bytes 2097152 | tf_op jit(solution)/shard_map/all_to_all | solution.py:254
  (38 other events, 113.0 us)
where the time goes:
time: 464 us; the launch traced here: 460 us
  local copies, waits for them, and re-layouts  130 us (28%)
  other arithmetic  100 us (22%)
  matrix products  76.1 us (16%)
  waiting for transfers between devices  65.8 us (14%)
  blocking collectives  47.4 us (10%)
  starting transfers between devices  31.9 us (7%)
  loops' own time  7.35 us (2%)
    psum x1, blocking collectives, on_device(): summed = lax.psum(spread, ('seq', 'dp'))  47.4 us
    scatter-add x8, other arithmetic, backward_one_group(): key_acc = key_acc.at[flat_links].add(key_part.reshape(-1, BLOCK, HEAD))  37.3 us
    scatter-add x8, other arithmetic, backward_one_group(): value_acc.at[flat_links].add(value_part.reshape(-1, BLOCK, HEAD))  37.3 us
    dynamic_slice x28, local copies, waits for them, and re-layouts, head_tiles(): picked = lax.dynamic_index_in_dim(array_in, head_index, 1, keepdims=False)  27.6 us
    dot_general x8, matrix products, gradients(): jnp.einsum('gqkb,gqe->gkbe', rounded, grad_tile, preferred_element_type=j...  24.4 us
    dot_general x8, matrix products, gradients(): jnp.einsum('gqkb,gqe->gkbe', grad_scores, queries, preferred_element_type...  22.2 us
    gather x8, local copies, waits for them, and re-layouts, backward_one_group(): value_tiles = value_all[chosen]  13.4 us
    dot_general x8, matrix products, gradients(): jnp.einsum('gqe,gkbe->gqkb', grad_tile, value_tiles, preferred_element_ty...  13 us
  transfers between devices with their start and end apart: 8, of which 6 were waited for; matrix products, arithmetic and copies ran while one was open for 52% of the time, Pallas kernels for 0%

commit v1 on v0

--- a/solution.py
+++ b/solution.py
@@ -1,10 +1,17 @@
+import functools
+
 import jax
 import jax.numpy as jnp
 from jax import lax
+from jax.experimental import pallas as pl
+from jax.experimental.pallas import tpu as pltpu
 from jax.sharding import PartitionSpec as P
+
+MESH = pl.DeviceIdType.MESH
 
 HEAD = 128
 BLOCK = 128
+CHUNK = 256
 
 
 tile_group = 4
@@ -210,7 +217,234 @@
     return lax.fori_loop(0, local_heads, backward_one_head, initial)
 
 
+def exchange_kernel(
+    n,
+    local_heads,
+    scaling,
+    query_ref,
+    key_ref,
+    value_ref,
+    grad_ref,
+    sink_ref,
+    attended_ref,
+    query_grad_ref,
+    key_grad_ref,
+    value_grad_ref,
+    sink_out_ref,
+    held,
+    made,
+    key_acc,
+    value_acc,
+    own_in,
+    own_out,
+    in_send,
+    in_recv,
+    out_send,
+    out_recv,
+):
+    me = lax.axis_index("seq")
+    rows = query_ref.shape[0]
+    total_rows = held.shape[2]
+    given = (query_ref, key_ref, value_ref, grad_ref)
+    wanted = (attended_ref, query_grad_ref, key_grad_ref, value_grad_ref)
+
+    def partner(step):
+        return lax.rem(me + step, n)
+
+    def columns(device, head):
+        return pl.ds(pl.multiple_of((device * local_heads + head) * HEAD, HEAD), HEAD)
+
+    def row_range(device):
+        return pl.ds(pl.multiple_of(device * rows, rows), rows)
+
+    def copies_in(head):
+        own, remote = [], []
+        for which, source in enumerate(given):
+            own.append(
+                pltpu.make_async_copy(
+                    source.at[:, columns(me, head)],
+                    held.at[which, head, row_range(me)],
+                    own_in.at[head, which],
+                )
+            )
+            for step in range(1, n):
+                to = partner(step)
+                remote.append(
+                    pltpu.make_async_remote_copy(
+                        src_ref=source.at[:, columns(to, head)],
+                        dst_ref=held.at[which, head, row_range(me)],
+                        send_sem=in_send.at[head, which, step - 1],
+                        recv_sem=in_recv.at[head, which, step - 1],
+                        device_id={"seq": to},
+                        device_id_type=MESH,
+                    )
+                )
+        return own, remote
+
+    def copies_out(head):
+        own, remote = [], []
+        for which, target in enumerate(wanted):
+            own.append(
+                pltpu.make_async_copy(
+                    made.at[which, head, row_range(me)],
+                    target.at[:, columns(me, head)],
+                    own_out.at[head, which],
+                )
+            )
+            for step in range(1, n):
+                to = partner(step)
+                remote.append(
+                    pltpu.make_async_remote_copy(
+                        src_ref=made.at[which, head, row_range(to)],
+                        dst_ref=target.at[:, columns(me, head)],
+                        send_sem=out_send.at[head, which, step - 1],
+                        recv_sem=out_recv.at[head, which, step - 1],
+                        device_id={"seq": to},
+                        device_id_type=MESH,
+                    )
+                )
+        return own, remote
+
+    def start_all(copies):
+        own, remote = copies
+        for copy in remote + own:
+            copy.start()
+
+    barrier = pltpu.get_barrier_semaphore()
+    for step in range(1, n):
+        pl.semaphore_signal(
+            barrier, inc=1, device_id={"seq": partner(step)}, device_id_type=MESH
+        )
+    pl.semaphore_wait(barrier, n - 1)
+
+    start_all(copies_in(0))
+    if local_heads > 1:
+        start_all(copies_in(1))
+    sink_out_ref[...] = jnp.zeros_like(sink_out_ref)
+    lanes = lax.broadcasted_iota(jnp.int32, sink_out_ref.shape, 1)
+
+    def one_head(head, carry):
+        own, remote = copies_in(head)
+        for copy in own:
+            copy.wait()
+        for copy in remote:
+            copy.wait_recv()
+
+        @pl.when(head + 2 < local_heads)
+        def _():
+            start_all(copies_in(head + 2))
+
+        sink_value = sink_ref[me * local_heads + head]
+        key_acc[...] = jnp.zeros_like(key_acc)
+        value_acc[...] = jnp.zeros_like(value_acc)
+
+        def one_chunk(chunk, sink_sum):
+            part = pl.ds(pl.multiple_of(chunk * CHUNK, CHUNK), CHUNK)
+            queries = held[0, head, part]
+            keys = held[1, head]
+            values = held[2, head]
+            grads = held[3, head, part]
+            scores = dot(queries, keys, 1, 1) * scaling
+            row_top = jnp.maximum(jnp.max(scores, axis=1, keepdims=True), sink_value)
+            raised = jnp.exp(scores - row_top)
+            sink_raised = jnp.exp(sink_value - row_top)
+            inverse = 1.0 / (jnp.sum(raised, axis=1, keepdims=True) + sink_raised)
+            weights = raised * inverse
+            rounded = weights.astype(jnp.bfloat16)
+            attended = dot(rounded, values, 1, 0).astype(jnp.bfloat16)
+            made[0, head, part] = attended
+            row_dot = jnp.sum(
+                grads.astype(jnp.float32) * attended.astype(jnp.float32), axis=1, keepdims=True
+            )
+            grad_weights = dot(grads, values, 1, 1)
+            grad_scores = (weights * (grad_weights - row_dot)).astype(jnp.bfloat16)
+            made[1, head, part] = (dot(grad_scores, keys, 1, 0) * scaling).astype(jnp.bfloat16)
+            value_acc[...] += dot(rounded, grads, 0, 0)
+            key_acc[...] += dot(grad_scores, queries, 0, 0)
+            terms = sink_raised * inverse * row_dot
+            return sink_sum + jnp.sum(terms, axis=0, keepdims=True)
+
+        sink_sum = lax.fori_loop(
+            0, total_rows // CHUNK, one_chunk, jnp.zeros((1, 1), jnp.float32)
+        )
+        made[2, head] = (key_acc[...] * scaling).astype(jnp.bfloat16)
+        made[3, head] = value_acc[...].astype(jnp.bfloat16)
+        start_all(copies_out(head))
+        sink_out_ref[...] = jnp.where(lanes == me * local_heads + head, -sink_sum, sink_out_ref[...])
+        return carry
+
+    lax.fori_loop(0, local_heads, one_head, 0)
+
+    def finish(head, carry):
+        for copy in copies_in(head)[1]:
+            copy.wait_send()
+        own, remote = copies_out(head)
+        for copy in own:
+            copy.wait()
+        for copy in remote:
+            copy.wait()
+        return carry
+
+    lax.fori_loop(0, local_heads, finish, 0)
+
+
+def dot(left, right, left_dim, right_dim):
+    return lax.dot_general(
+        left,
+        right,
+        (((left_dim,), (right_dim,)), ((), ())),
+        preferred_element_type=jnp.float32,
+    )
+
+
+def every_block(query_rows, key_rows, value_rows, sink_logit, grad_out):
+    token_count = query_rows.shape[1]
+    head_count = sink_logit.shape[0]
+    n = lax.axis_size("seq")
+    local_heads = head_count // n
+    total_rows = n * token_count
+    width = head_count * HEAD
+    anywhere = pl.BlockSpec(memory_space=pl.ANY)
+    result = jax.ShapeDtypeStruct((token_count, width), jnp.bfloat16)
+    outs = pl.pallas_call(
+        functools.partial(exchange_kernel, n, local_heads, HEAD ** (-0.5)),
+        out_shape=(result,) * 4 + (jax.ShapeDtypeStruct((8, 128), jnp.float32),),
+        in_specs=[anywhere] * 4 + [pl.BlockSpec(memory_space=pltpu.SMEM)],
+        out_specs=(anywhere,) * 4 + (pl.BlockSpec(memory_space=pltpu.VMEM),),
+        scratch_shapes=[
+            pltpu.VMEM((4, local_heads, total_rows, HEAD), jnp.bfloat16),
+            pltpu.VMEM((4, local_heads, total_rows, HEAD), jnp.bfloat16),
+            pltpu.VMEM((total_rows, HEAD), jnp.float32),
+            pltpu.VMEM((total_rows, HEAD), jnp.float32),
+            pltpu.SemaphoreType.DMA((local_heads, 4)),
+            pltpu.SemaphoreType.DMA((local_heads, 4)),
+            pltpu.SemaphoreType.DMA((local_heads, 4, n - 1)),
+            pltpu.SemaphoreType.DMA((local_heads, 4, n - 1)),
+            pltpu.SemaphoreType.DMA((local_heads, 4, n - 1)),
+            pltpu.SemaphoreType.DMA((local_heads, 4, n - 1)),
+        ],
+        compiler_params=pltpu.CompilerParams(
+            collective_id=0, has_side_effects=True, vmem_limit_bytes=48 * 1024 * 1024
+        ),
+        cost_estimate=pl.CostEstimate(
+            flops=12 * local_heads * total_rows * total_rows * HEAD,
+            bytes_accessed=16 * token_count * width,
+            transcendentals=local_heads * total_rows * total_rows,
+        ),
+    )(
+        query_rows.reshape(token_count, width),
+        key_rows.reshape(token_count, width),
+        value_rows.reshape(token_count, width),
+        grad_out.reshape(token_count, width),
+        sink_logit,
+    )
+    summed = lax.psum(outs[4][0, :head_count], ("seq", "dp"))
+    return tuple(out[None] for out in outs[:4]) + (summed / lax.axis_size("dp"),)
+
+
 def on_device(query_rows, key_rows, value_rows, sink_logit, grad_out, pattern):
+    if pattern.shape[1] == pattern.shape[2]:
+        return every_block(query_rows, key_rows, value_rows, sink_logit, grad_out)
     token_count = query_rows.shape[1]
     head_count = sink_logit.shape[0]
     local_heads = head_count // lax.axis_size("seq")

time: 464 us -> 147 us (0.32)
  local copies, waits for them, and re-layouts: 130 us -> 8.05 us
  other arithmetic: 100 us -> 0.51 us
  Pallas kernels: 0 us -> 97.3 us
  matrix products: 76.1 us -> 0 us
  waiting for transfers between devices: 65.8 us -> 0 us
  starting transfers between devices: 31.9 us -> 0 us
  loops' own time: 7.35 us -> 0 us
  blocking collectives: 47.4 us -> 40.3 us
    pallas_call x0 -> x1, Pallas kernels: none -> 97.3 us  [every_block(): pl.pallas_call(functools.partial(exchange_kernel, n, local_heads, HEAD **...]
    dot_general x56 -> x0, matrix products: 76.1 us -> none  [the longest x8 24.4 us: gradients(): jnp.einsum('gqkb,gqe->gkbe', rounded, grad_tile, preferred_element_type=j...]
    scatter-add x16 -> x0, other arithmetic: 74.6 us -> none  [the longest x8 37.3 us: backward_one_group(): key_acc = key_acc.at[flat_links].add(key_part.reshape(-1, BLOCK, HEAD))]
    all_to_all x8 -> x0, waiting for transfers between devices: 65.8 us -> none  [the longest x1 12.3 us: on_device(): lax.all_to_all(split_heads(query_rows), 'seq', split_axis=1, concat_axis=...]
    dynamic_slice x38 -> x0, local copies, waits for them, and re-layouts: 32.6 us -> none  [the longest x28 27.6 us: head_tiles(): picked = lax.dynamic_index_in_dim(array_in, head_index, 1, keepdims=False)]
    all_to_all x8 -> x0, starting transfers between devices: 31.9 us -> none  [the longest x1 5.16 us: on_device(): lax.all_to_all(split_heads(query_rows), 'seq', split_axis=1, concat_axis=...]
    gather x32 -> x0, local copies, waits for them, and re-layouts: 31.4 us -> none  [the longest x8 13.4 us: backward_one_group(): value_tiles = value_all[chosen]]
    while x180 -> x0, local copies, waits for them, and re-layouts: 16.2 us -> none  [the longest x3 6.69 us: backward_pass(): return lax.fori_loop(0, local_heads, backward_one_head, initial)]
  transfers between devices with their start and end apart: 8 -> 0, of which waited for: 6 -> 0; matrix products, arithmetic and copies ran while one was open for 52% -> 0% of each run, Pallas kernels for 0% -> 0%
where the time goes in v1:
time: 147 us
  Pallas kernels  97.3 us (66%)
  blocking collectives  40.3 us (27%)
  local copies, waits for them, and re-layouts  8.05 us (5%)
    pallas_call x1, Pallas kernels, every_block(): pl.pallas_call(functools.partial(exchange_kernel, n, local_heads, HEAD **...  97.3 us
    psum x1, blocking collectives, every_block(): summed = lax.psum(outs[4][0, :head_count], ('seq', 'dp'))  40.3 us
    unnamed x10, local copies, waits for them, and re-layouts  8.05 us

profile of v1, /device:TPU:0, one launch (start us, length us, event | category | flops | bytes accessed | tf_op | source)
XLA Modules:
  0.0 146.9 jit_solution(16665023234250633369)
XLA Ops:
  0.6 0.0 copy-start.2
  0.6 0.6 copy-done.2
  1.3 0.0 copy-start.1
  1.3 1.2 copy-done.1
  2.5 97.3 %shard_map.92 = (bf16[256,2048]{1,0:T(8,128)(2,1)S(1)}, bf16[256,2048]{1,0:T(8,128)(2,1)S(1)}, bf16[256,2048]{1,0:T(8,128)(2,1)S(1)}, bf16[256,2048]{1,0:T(8,128)(2,1)S(1)}, f32[8,128]{1,0:T(8,128)S(1)}) custom-call(bf16[256,2048]{1,0:T(8,128)(2,1)S(1)} %bitcast.14, bf16[256,2048]{1,0:T(8,128)(2,1)} %bitcast.15, bf16[256,2048]{1,0:T(8,128)(2,1)} %bitcast.16, ...), custom_call_target="tpu_custom_call" | custom-call | flops 6442450944 | bytes 8388608 | tf_op jit(solution)/shard_map/pallas_call | solution.py:409
  99.8 0.0 copy-start
  99.8 1.0 copy-done
  100.8 40.3 %psum.7 = f32[16]{0:T(128)S(1)} all-reduce(f32[16]{0:T(128)S(1)} %slice_bitcast_fusion), channel_id=1, replica_groups=mesh['seq'=4,'dp'=8] {'seq','dp'}, use_global_device_ids=true, to_apply=%region_0.0 | all-reduce | flops 16 | bytes 128 | tf_op jit(solution)/shard_map/psum | solution.py:441
  141.1 0.5 broadcast_multiply_fusion
  141.7 2.3 %copy.14 = bf16[1,256,2048]{2,1,0:T(8,128)(2,1)} copy(bf16[1,256,2048]{2,1,0:T(8,128)(2,1)} %bitcast.13) | data formatting | bytes 2097152
  144.0 1.0 copy.15
  144.9 1.0 copy.16
  145.9 1.0 copy.17
  (1 shorter events, 0.0 us)
Async XLA Ops:
  0.6 0.7 copy-start.2
  1.3 1.2 copy-start.1
  99.8 1.0 copy-start

commit v2 on v1

--- a/solution.py
+++ b/solution.py
@@ -219,6 +219,7 @@
 
 def exchange_kernel(
     n,
+    documents,
     local_heads,
     scaling,
     query_ref,
@@ -235,14 +236,23 @@
     made,
     key_acc,
     value_acc,
+    sink_values,
+    sink_terms,
+    sink_totals,
+    sink_copy,
     own_in,
     own_out,
     in_send,
     in_recv,
     out_send,
     out_recv,
+    terms_send,
+    terms_recv,
+    totals_send,
+    totals_recv,
 ):
     me = lax.axis_index("seq")
+    document = lax.axis_index("dp")
     rows = query_ref.shape[0]
     total_rows = held.shape[2]
     given = (query_ref, key_ref, value_ref, grad_ref)
@@ -310,18 +320,50 @@
         for copy in remote + own:
             copy.start()
 
+    def terms_copies():
+        return [
+            pltpu.make_async_remote_copy(
+                src_ref=sink_terms.at[document],
+                dst_ref=sink_terms.at[document],
+                send_sem=terms_send.at[step - 1],
+                recv_sem=terms_recv.at[step - 1],
+                device_id={"dp": lax.rem(document + step, documents)},
+                device_id_type=MESH,
+            )
+            for step in range(1, documents)
+        ]
+
+    def totals_copies():
+        return [
+            pltpu.make_async_remote_copy(
+                src_ref=sink_totals.at[me],
+                dst_ref=sink_totals.at[me],
+                send_sem=totals_send.at[step - 1],
+                recv_sem=totals_recv.at[step - 1],
+                device_id={"seq": partner(step)},
+                device_id_type=MESH,
+            )
+            for step in range(1, n)
+        ]
+
+    sinks_in = pltpu.make_async_copy(sink_ref, sink_values, sink_copy)
+    sinks_in.start()
     barrier = pltpu.get_barrier_semaphore()
     for step in range(1, n):
         pl.semaphore_signal(
             barrier, inc=1, device_id={"seq": partner(step)}, device_id_type=MESH
         )
-    pl.semaphore_wait(barrier, n - 1)
+    for step in range(1, documents):
+        other = lax.rem(document + step, documents)
+        pl.semaphore_signal(barrier, inc=1, device_id={"dp": other}, device_id_type=MESH)
+    pl.semaphore_wait(barrier, n + documents - 2)
 
     start_all(copies_in(0))
     if local_heads > 1:
         start_all(copies_in(1))
-    sink_out_ref[...] = jnp.zeros_like(sink_out_ref)
+    sink_terms[document] = jnp.zeros(sink_out_ref.shape, jnp.float32)
     lanes = lax.broadcasted_iota(jnp.int32, sink_out_ref.shape, 1)
+    sinks_in.wait()
 
     def one_head(head, carry):
         own, remote = copies_in(head)
@@ -334,7 +376,7 @@
         def _():
             start_all(copies_in(head + 2))
 
-        sink_value = sink_ref[me * local_heads + head]
+        sink_value = sink_values[me * local_heads + head]
         key_acc[...] = jnp.zeros_like(key_acc)
         value_acc[...] = jnp.zeros_like(value_acc)
 
@@ -369,11 +411,28 @@
         )
         made[2, head] = (key_acc[...] * scaling).astype(jnp.bfloat16)
         made[3, head] = value_acc[...].astype(jnp.bfloat16)
+        sink_terms[document] = jnp.where(
+            lanes == me * local_heads + head, -sink_sum, sink_terms[document]
+        )
+
+        @pl.when(head == local_heads - 1)
+        def _():
+            for copy in terms_copies():
+                copy.start()
+
         start_all(copies_out(head))
-        sink_out_ref[...] = jnp.where(lanes == me * local_heads + head, -sink_sum, sink_out_ref[...])
         return carry
 
     lax.fori_loop(0, local_heads, one_head, 0)
+
+    for copy in terms_copies():
+        copy.wait()
+    sink_totals[me] = jnp.sum(sink_terms[...], axis=0)
+    for copy in totals_copies():
+        copy.start()
+    for copy in totals_copies():
+        copy.wait()
+    sink_out_ref[...] = jnp.sum(sink_totals[...], axis=0) * (1.0 / documents)
 
     def finish(head, carry):
         for copy in copies_in(head)[1]:
@@ -388,6 +447,25 @@
     lax.fori_loop(0, local_heads, finish, 0)
 
 
+def store_kernel(*refs):
+    sources, sink_ref, targets, sink_out_ref, done = refs[:4], refs[4], refs[5:9], refs[9], refs[10]
+    rows = sources[0].shape[0] // 2
+    copies = [
+        pltpu.make_async_copy(
+            source.at[pl.ds(half * rows, rows)],
+            target.at[pl.ds(half * rows, rows)],
+            done.at[which, half],
+        )
+        for which, (source, target) in enumerate(zip(sources, targets))
+        for half in range(2)
+    ]
+    for copy in copies:
+        copy.start()
+    sink_out_ref[...] = sink_ref[0, : sink_out_ref.shape[0]]
+    for copy in copies:
+        copy.wait()
+
+
 def dot(left, right, left_dim, right_dim):
     return lax.dot_general(
         left,
@@ -404,24 +482,35 @@
     local_heads = head_count // n
     total_rows = n * token_count
     width = head_count * HEAD
+    documents = lax.axis_size("dp")
     anywhere = pl.BlockSpec(memory_space=pl.ANY)
+    in_hbm = pl.BlockSpec(memory_space=pltpu.HBM)
+    in_vmem = pl.BlockSpec(memory_space=pltpu.VMEM)
     result = jax.ShapeDtypeStruct((token_count, width), jnp.bfloat16)
     outs = pl.pallas_call(
-        functools.partial(exchange_kernel, n, local_heads, HEAD ** (-0.5)),
+        functools.partial(exchange_kernel, n, documents, local_heads, HEAD ** (-0.5)),
         out_shape=(result,) * 4 + (jax.ShapeDtypeStruct((8, 128), jnp.float32),),
-        in_specs=[anywhere] * 4 + [pl.BlockSpec(memory_space=pltpu.SMEM)],
-        out_specs=(anywhere,) * 4 + (pl.BlockSpec(memory_space=pltpu.VMEM),),
+        in_specs=[in_hbm] * 5,
+        out_specs=(anywhere,) * 4 + (in_vmem,),
         scratch_shapes=[
             pltpu.VMEM((4, local_heads, total_rows, HEAD), jnp.bfloat16),
             pltpu.VMEM((4, local_heads, total_rows, HEAD), jnp.bfloat16),
             pltpu.VMEM((total_rows, HEAD), jnp.float32),
             pltpu.VMEM((total_rows, HEAD), jnp.float32),
+            pltpu.SMEM((head_count,), jnp.float32),
+            pltpu.VMEM((documents, 8, 128), jnp.float32),
+            pltpu.VMEM((n, 8, 128), jnp.float32),
+            pltpu.SemaphoreType.DMA,
             pltpu.SemaphoreType.DMA((local_heads, 4)),
             pltpu.SemaphoreType.DMA((local_heads, 4)),
             pltpu.SemaphoreType.DMA((local_heads, 4, n - 1)),
             pltpu.SemaphoreType.DMA((local_heads, 4, n - 1)),
             pltpu.SemaphoreType.DMA((local_heads, 4, n - 1)),
             pltpu.SemaphoreType.DMA((local_heads, 4, n - 1)),
+            pltpu.SemaphoreType.DMA((documents - 1,)),
+            pltpu.SemaphoreType.DMA((documents - 1,)),
+            pltpu.SemaphoreType.DMA((n - 1,)),
+            pltpu.SemaphoreType.DMA((n - 1,)),
         ],
         compiler_params=pltpu.CompilerParams(
             collective_id=0, has_side_effects=True, vmem_limit_bytes=48 * 1024 * 1024
@@ -438,8 +527,15 @@
         grad_out.reshape(token_count, width),
         sink_logit,
     )
-    summed = lax.psum(outs[4][0, :head_count], ("seq", "dp"))
-    return tuple(out[None] for out in outs[:4]) + (summed / lax.axis_size("dp"),)
+    stored = pl.pallas_call(
+        store_kernel,
+        out_shape=(result,) * 4 + (jax.ShapeDtypeStruct((head_count,), jnp.float32),),
+        in_specs=[anywhere] * 4 + [in_vmem],
+        out_specs=(in_hbm,) * 4 + (in_vmem,),
+        scratch_shapes=[pltpu.SemaphoreType.DMA((4, 2))],
+        compiler_params=pltpu.CompilerParams(vmem_limit_bytes=4 * 1024 * 1024),
+    )(*outs)
+    return tuple(out[None] for out in stored[:4]) + (stored[4],)
 
 
 def on_device(query_rows, key_rows, value_rows, sink_logit, grad_out, pattern):

time: 147 us -> 106 us (0.72)
  blocking collectives: 40.3 us -> 0 us
  Pallas kernels: 97.3 us -> 104 us
  local copies, waits for them, and re-layouts: 8.05 us -> 1.87 us
    psum x1 -> x0, blocking collectives: 40.3 us -> none  [every_block(): summed = lax.psum(outs[4][0, :head_count], ('seq', 'dp'))]
    pallas_call x1 -> x2, Pallas kernels: 97.3 us -> 104 us  [the longest x1 101 us: every_block(): pl.pallas_call(functools.partial(exchange_kernel, n, documents, local_hea...]
    unnamed x10 -> x4, local copies, waits for them, and re-layouts: 8.05 us -> 1.87 us
where the time goes in v2:
time: 106 us
  Pallas kernels  104 us (98%)
  local copies, waits for them, and re-layouts  1.87 us (2%)
    pallas_call x1, Pallas kernels, every_block(): pl.pallas_call(functools.partial(exchange_kernel, n, documents, local_hea...  101 us
    pallas_call x1, Pallas kernels, every_block(): pl.pallas_call(store_kernel, out_shape=(result,) * 4 + (jax.ShapeDtypeStr...  2.58 us

profile of v2, /device:TPU:0, one launch (start us, length us, event | category | flops | bytes accessed | tf_op | source)
XLA Modules:
  0.0 106.1 jit_solution(7801882182626172267)
XLA Ops:
  0.6 0.0 copy-start.1
  0.6 0.6 copy-done.1
  1.3 0.0 copy-start
  1.3 1.2 %copy-done = bf16[1,256,2048]{2,1,0:T(8,128)(2,1)S(1)} copy-done((bf16[1,256,2048]{2,1,0:T(8,128)(2,1)S(1)}, bf16[1,256,2048]{2,1,0:T(8,128)(2,1)}, u32[]{:S(2)}) %copy-start) | copy-done | bytes 1048600
  2.5 101.0 %shard_map.92 = (bf16[256,2048]{1,0:T(8,128)(2,1)S(1)}, bf16[256,2048]{1,0:T(8,128)(2,1)S(1)}, bf16[256,2048]{1,0:T(8,128)(2,1)S(1)}, bf16[256,2048]{1,0:T(8,128)(2,1)S(1)}, f32[8,128]{1,0:T(8,128)S(1)}) custom-call(bf16[256,2048]{1,0:T(8,128)(2,1)S(1)} %bitcast.8, bf16[256,2048]{1,0:T(8,128)(2,1)} %bitcast.9, bf16[256,2048]{1,0:T(8,128)(2,1)} %bitcast.10, ...), custom_call_target="tpu_custom_call" | custom-call | flops 6442450944 | bytes 8388608 | tf_op jit(solution)/shard_map/pallas_call | solution.py:490
  103.5 2.6 %shard_map.93 = (bf16[256,2048]{1,0:T(8,128)(2,1)}, bf16[256,2048]{1,0:T(8,128)(2,1)}, bf16[256,2048]{1,0:T(8,128)(2,1)}, bf16[256,2048]{1,0:T(8,128)(2,1)}, f32[16]{0:T(128)}) custom-call(bf16[256,2048]{1,0:T(8,128)(2,1)S(1)} %get-tuple-element.15.refs_0_, bf16[256,2048]{1,0:T(8,128)(2,1)S(1)} %get-tuple-element.16.refs_1_, ...), custom_call_target="tpu_custom_call" | custom-call | tf_op jit(solution)/shard_map/pallas_call | solution.py:530
Async XLA Ops:
  0.6 0.7 copy-start.1
  1.3 1.2 %copy-start = (bf16[1,256,2048]{2,1,0:T(8,128)(2,1)S(1)}, bf16[1,256,2048]{2,1,0:T(8,128)(2,1)}, u32[]{:S(2)}) copy-start(bf16[1,256,2048]{2,1,0:T(8,128)(2,1)} %param.6) | copy-start | bytes 3145732

commit v3 on v2

--- a/solution.py
+++ b/solution.py
@@ -11,7 +11,6 @@
 
 HEAD = 128
 BLOCK = 128
-CHUNK = 256
 
 
 tile_group = 4
@@ -267,9 +266,10 @@
     def row_range(device):
         return pl.ds(pl.multiple_of(device * rows, rows), rows)
 
-    def copies_in(head):
+    def copies_in(head, pair):
         own, remote = [], []
-        for which, source in enumerate(given):
+        for which in (2 * pair, 2 * pair + 1):
+            source = given[which]
             own.append(
                 pltpu.make_async_copy(
                     source.at[:, columns(me, head)],
@@ -291,29 +291,23 @@
                 )
         return own, remote
 
-    def copies_out(head):
-        own, remote = [], []
-        for which, target in enumerate(wanted):
-            own.append(
-                pltpu.make_async_copy(
-                    made.at[which, head, row_range(me)],
-                    target.at[:, columns(me, head)],
-                    own_out.at[head, which],
-                )
-            )
-            for step in range(1, n):
-                to = partner(step)
-                remote.append(
-                    pltpu.make_async_remote_copy(
-                        src_ref=made.at[which, head, row_range(to)],
-                        dst_ref=target.at[:, columns(me, head)],
-                        send_sem=out_send.at[head, which, step - 1],
-                        recv_sem=out_recv.at[head, which, step - 1],
-                        device_id={"seq": to},
-                        device_id_type=MESH,
-                    )
-                )
-        return own, remote
+    def own_copy(which, head):
+        return pltpu.make_async_copy(
+            made.at[which, head, row_range(me)],
+            wanted[which].at[:, columns(me, head)],
+            own_out.at[head, which],
+        )
+
+    def copy_out(which, head, step):
+        to = partner(step)
+        return pltpu.make_async_remote_copy(
+            src_ref=made.at[which, head, row_range(to)],
+            dst_ref=wanted[which].at[:, columns(me, head)],
+            send_sem=out_send.at[head, which, step - 1],
+            recv_sem=out_recv.at[head, which, step - 1],
+            device_id={"seq": to},
+            device_id_type=MESH,
+        )
 
     def start_all(copies):
         own, remote = copies
@@ -358,30 +352,40 @@
         pl.semaphore_signal(barrier, inc=1, device_id={"dp": other}, device_id_type=MESH)
     pl.semaphore_wait(barrier, n + documents - 2)
 
-    start_all(copies_in(0))
-    if local_heads > 1:
-        start_all(copies_in(1))
+    start_all(copies_in(0, 0))
+    start_all(copies_in(0, 1))
     sink_terms[document] = jnp.zeros(sink_out_ref.shape, jnp.float32)
     lanes = lax.broadcasted_iota(jnp.int32, sink_out_ref.shape, 1)
     sinks_in.wait()
 
     def one_head(head, carry):
-        own, remote = copies_in(head)
-        for copy in own:
-            copy.wait()
-        for copy in remote:
-            copy.wait_recv()
+        for pair in range(2):
+            own, remote = copies_in(head, pair)
+            for copy in own:
+                copy.wait()
+            for copy in remote:
+                copy.wait_recv()
+
+            if pair == 0 and local_heads > 1:
+
+                @pl.when(head == 0)
+                def _():
+                    start_all(copies_in(1, 0))
+
+        @pl.when(head + 1 < local_heads)
+        def _():
+            start_all(copies_in(head + 1, 1))
 
         @pl.when(head + 2 < local_heads)
         def _():
-            start_all(copies_in(head + 2))
+            start_all(copies_in(head + 2, 0))
 
         sink_value = sink_values[me * local_heads + head]
         key_acc[...] = jnp.zeros_like(key_acc)
         value_acc[...] = jnp.zeros_like(value_acc)
 
-        def one_chunk(chunk, sink_sum):
-            part = pl.ds(pl.multiple_of(chunk * CHUNK, CHUNK), CHUNK)
+        def one_chunk(step, sink_sum):
+            part = row_range(partner(step))
             queries = held[0, head, part]
             keys = held[1, head]
             values = held[2, head]
@@ -401,13 +405,19 @@
             grad_weights = dot(grads, values, 1, 1)
             grad_scores = (weights * (grad_weights - row_dot)).astype(jnp.bfloat16)
             made[1, head, part] = (dot(grad_scores, keys, 1, 0) * scaling).astype(jnp.bfloat16)
+
+            @pl.when(step < n)
+            def _():
+                for which in range(2):
+                    copy_out(which, head, step).start()
+
             value_acc[...] += dot(rounded, grads, 0, 0)
             key_acc[...] += dot(grad_scores, queries, 0, 0)
             terms = sink_raised * inverse * row_dot
             return sink_sum + jnp.sum(terms, axis=0, keepdims=True)
 
         sink_sum = lax.fori_loop(
-            0, total_rows // CHUNK, one_chunk, jnp.zeros((1, 1), jnp.float32)
+            1, n + 1, one_chunk, jnp.zeros((1, 1), jnp.float32)
         )
         made[2, head] = (key_acc[...] * scaling).astype(jnp.bfloat16)
         made[3, head] = value_acc[...].astype(jnp.bfloat16)
@@ -420,7 +430,11 @@
             for copy in terms_copies():
                 copy.start()
 
-        start_all(copies_out(head))
+        for which in range(2, 4):
+            for step in range(1, n):
+                copy_out(which, head, step).start()
+        for which in range(4):
+            own_copy(which, head).start()
         return carry
 
     lax.fori_loop(0, local_heads, one_head, 0)
@@ -435,13 +449,13 @@
     sink_out_ref[...] = jnp.sum(sink_totals[...], axis=0) * (1.0 / documents)
 
     def finish(head, carry):
-        for copy in copies_in(head)[1]:
-            copy.wait_send()
-        own, remote = copies_out(head)
-        for copy in own:
-            copy.wait()
-        for copy in remote:
-            copy.wait()
+        for pair in range(2):
+            for copy in copies_in(head, pair)[1]:
+                copy.wait_send()
+        for which in range(4):
+            own_copy(which, head).wait()
+            for step in range(1, n):
+                copy_out(which, head, step).wait()
         return carry
 
     lax.fori_loop(0, local_heads, finish, 0)
@@ -513,7 +527,7 @@
             pltpu.SemaphoreType.DMA((n - 1,)),
         ],
         compiler_params=pltpu.CompilerParams(
-            collective_id=0, has_side_effects=True, vmem_limit_bytes=48 * 1024 * 1024
+            collective_id=0, has_side_effects=True, vmem_limit_bytes=49 * 1024 * 1024
         ),
         cost_estimate=pl.CostEstimate(
             flops=12 * local_heads * total_rows * total_rows * HEAD,

time: 106 us -> 105 us (level)
  local copies, waits for them, and re-layouts: 1.87 us -> 0.65 us
    unnamed x4 -> x2, local copies, waits for them, and re-layouts: 1.87 us -> 0.65 us
where the time goes in v3:
time: 105 us
  Pallas kernels  104 us (99%)
    pallas_call x1, Pallas kernels, every_block(): pl.pallas_call(functools.partial(exchange_kernel, n, documents, local_hea...  101 us
    pallas_call x1, Pallas kernels, every_block(): pl.pallas_call(store_kernel, out_shape=(result,) * 4 + (jax.ShapeDtypeStr...  2.58 us

profile of v3, /device:TPU:0, one launch (start us, length us, event | category | flops | bytes accessed | tf_op | source)
XLA Modules:
  0.0 105.2 jit_solution(2252986319369293675)
XLA Ops:
  0.6 0.0 copy-start
  0.6 0.6 copy-done
  1.3 101.4 %shard_map.92 = (bf16[256,2048]{1,0:T(8,128)(2,1)S(1)}, bf16[256,2048]{1,0:T(8,128)(2,1)S(1)}, bf16[256,2048]{1,0:T(8,128)(2,1)S(1)}, bf16[256,2048]{1,0:T(8,128)(2,1)S(1)}, f32[8,128]{1,0:T(8,128)S(1)}) custom-call(bf16[256,2048]{1,0:T(8,128)(2,1)} %bitcast.8, bf16[256,2048]{1,0:T(8,128)(2,1)} %bitcast.9, bf16[256,2048]{1,0:T(8,128)(2,1)} %bitcast.10, ...), custom_call_target="tpu_custom_call" | custom-call | flops 6442450944 | bytes 8388608 | tf_op jit(solution)/shard_map/pallas_call | solution.py:504
  102.7 2.6 %shard_map.93 = (bf16[256,2048]{1,0:T(8,128)(2,1)}, bf16[256,2048]{1,0:T(8,128)(2,1)}, bf16[256,2048]{1,0:T(8,128)(2,1)}, bf16[256,2048]{1,0:T(8,128)(2,1)}, f32[16]{0:T(128)}) custom-call(bf16[256,2048]{1,0:T(8,128)(2,1)S(1)} %get-tuple-element.15.refs_0_, bf16[256,2048]{1,0:T(8,128)(2,1)S(1)} %get-tuple-element.16.refs_1_, ...), custom_call_target="tpu_custom_call" | custom-call | tf_op jit(solution)/shard_map/pallas_call | solution.py:544
Async XLA Ops:
  0.6 0.7 copy-start

commit v4 on v3

--- a/solution.py
+++ b/solution.py
@@ -463,7 +463,7 @@
 
 def store_kernel(*refs):
     sources, sink_ref, targets, sink_out_ref, done = refs[:4], refs[4], refs[5:9], refs[9], refs[10]
-    rows = sources[0].shape[0] // 2
+    rows = sources[0].shape[0] // 4
     copies = [
         pltpu.make_async_copy(
             source.at[pl.ds(half * rows, rows)],
@@ -471,7 +471,7 @@
             done.at[which, half],
         )
         for which, (source, target) in enumerate(zip(sources, targets))
-        for half in range(2)
+        for half in range(4)
     ]
     for copy in copies:
         copy.start()
@@ -546,7 +546,7 @@
         out_shape=(result,) * 4 + (jax.ShapeDtypeStruct((head_count,), jnp.float32),),
         in_specs=[anywhere] * 4 + [in_vmem],
         out_specs=(in_hbm,) * 4 + (in_vmem,),
-        scratch_shapes=[pltpu.SemaphoreType.DMA((4, 2))],
+        scratch_shapes=[pltpu.SemaphoreType.DMA((4, 4))],
         compiler_params=pltpu.CompilerParams(vmem_limit_bytes=4 * 1024 * 1024),
     )(*outs)
     return tuple(out[None] for out in stored[:4]) + (stored[4],)

time: 105 us -> 105 us (level)
  no operation moved by 1% of the time
where the time goes in v4:
time: 105 us
  Pallas kernels  104 us (99%)
    pallas_call x1, Pallas kernels, every_block(): pl.pallas_call(functools.partial(exchange_kernel, n, documents, local_hea...  101 us
    pallas_call x1, Pallas kernels, every_block(): pl.pallas_call(store_kernel, out_shape=(result,) * 4 + (jax.ShapeDtypeStr...  2.65 us

profile of v4, /device:TPU:0, one launch (start us, length us, event | category | flops | bytes accessed | tf_op | source)
XLA Modules:
  0.0 105.3 jit_solution(8388744150970280467)
XLA Ops:
  0.6 0.0 copy-start
  0.6 0.6 copy-done
  1.3 101.4 %shard_map.92 = (bf16[256,2048]{1,0:T(8,128)(2,1)S(1)}, bf16[256,2048]{1,0:T(8,128)(2,1)S(1)}, bf16[256,2048]{1,0:T(8,128)(2,1)S(1)}, bf16[256,2048]{1,0:T(8,128)(2,1)S(1)}, f32[8,128]{1,0:T(8,128)S(1)}) custom-call(bf16[256,2048]{1,0:T(8,128)(2,1)} %bitcast.8, bf16[256,2048]{1,0:T(8,128)(2,1)} %bitcast.9, bf16[256,2048]{1,0:T(8,128)(2,1)} %bitcast.10, ...), custom_call_target="tpu_custom_call" | custom-call | flops 6442450944 | bytes 8388608 | tf_op jit(solution)/shard_map/pallas_call | solution.py:504
  102.7 2.6 %shard_map.93 = (bf16[256,2048]{1,0:T(8,128)(2,1)}, bf16[256,2048]{1,0:T(8,128)(2,1)}, bf16[256,2048]{1,0:T(8,128)(2,1)}, bf16[256,2048]{1,0:T(8,128)(2,1)}, f32[16]{0:T(128)}) custom-call(bf16[256,2048]{1,0:T(8,128)(2,1)S(1)} %get-tuple-element.15.refs_0_, bf16[256,2048]{1,0:T(8,128)(2,1)S(1)} %get-tuple-element.16.refs_1_, ...), custom_call_target="tpu_custom_call" | custom-call | tf_op jit(solution)/shard_map/pallas_call | solution.py:544
Async XLA Ops:
  0.6 0.7 copy-start
